TPU v7x, 32 devices: a whole 2x2x4 slice. The times are simulated.
32 devices in a mesh: fsdp: 2 (over x), ctx: 4 (over z), tp: 4 (over y, core).
Axes of the slice: x: 2, y: 2, z: 4, core: 2. Of those that a mesh axis runs over, the one named last changes fastest.
Arguments:
- tokens: bfloat16 [3072, 512], P(('fsdp', 'ctx'), 'tp'), may hold values from -62 to 62
- first_expand: bfloat16 [512, 2048], P(('fsdp', 'ctx'), 'tp'), may hold values from -0.25 to 0.25
- first_shrink: bfloat16 [2048, 512], P('tp', ('fsdp', 'ctx')), may hold values from -0.25 to 0.25
- attend_input: bfloat16 [512, 3, 512], P(('fsdp', 'ctx'), None, 'tp'), may hold values from -0.25 to 0.25
- position_map: bfloat16 [512, 512], P(('fsdp', 'ctx'), 'tp'), may hold values from -0.25 to 0.25
- position_bias: float32 [2, 8, 64], P(None, 'tp'), may hold values from -4 to 4
- attend_output: bfloat16 [512, 512], P('tp', ('fsdp', 'ctx')), may hold values from -2.5 to 2.5
- gating_map: bfloat16 [512, 2, 512], P(('fsdp', 'ctx'), None, 'tp'), may hold values from -0.25 to 0.25
- depth_kernel: float32 [31, 512], P(None, 'tp'), may hold values from -1 to 1
- batch_scale: float32 [512], P('tp'), may hold values from 0.1 to 1.9
- batch_shift: float32 [512], P('tp'), may hold values from -3 to 3
- mixing_map: bfloat16 [512, 512], P('tp', ('fsdp', 'ctx')), may hold values from -0.25 to 0.25
- second_expand: bfloat16 [512, 2048], P(('fsdp', 'ctx'), 'tp'), may hold values from -0.25 to 0.25
- second_shrink: bfloat16 [2048, 512], P('tp', ('fsdp', 'ctx')), may hold values from -0.25 to 0.25
- layer_gains: float32 [5, 512], P(None, 'tp'), may hold values from 0.1 to 1.9
- cotangent: bfloat16 [3072, 512], P(('fsdp', 'ctx'), 'tp'), may hold values from -6 to 6
Outputs:
- outputs: bfloat16 [3072, 512], P(('fsdp', 'ctx'), 'tp')
- tokens_grad: float32 [3072, 512], P(('fsdp', 'ctx'), 'tp')
- first_expand_grad: float32 [512, 2048], P(('fsdp', 'ctx'), 'tp')
- first_shrink_grad: float32 [2048, 512], P('tp', ('fsdp', 'ctx'))
- attend_input_grad: float32 [512, 3, 512], P(('fsdp', 'ctx'), None, 'tp')
- position_map_grad: float32 [512, 512], P(('fsdp', 'ctx'), 'tp')
- position_bias_grad: float32 [2, 8, 64], P(None, 'tp')
- attend_output_grad: float32 [512, 512], P('tp', ('fsdp', 'ctx'))
- gating_map_grad: float32 [512, 2, 512], P(('fsdp', 'ctx'), None, 'tp')
- depth_kernel_grad: float32 [31, 512], P(None, 'tp')
- batch_scale_grad: float32 [512], P('tp')
- batch_shift_grad: float32 [512], P('tp')
- mixing_map_grad: float32 [512, 512], P('tp', ('fsdp', 'ctx'))
- second_expand_grad: float32 [512, 2048], P(('fsdp', 'ctx'), 'tp')
- second_shrink_grad: float32 [2048, 512], P('tp', ('fsdp', 'ctx'))
- layer_gains_grad: float32 [5, 512], P(None, 'tp')
All inputs are finite; a program needn't handle non-finite values.
Results may differ from a plain program's by a relative error of at most 0.04.
Values may be sent and summed in bfloat16 or wider, within the bound.
No kernel may reach another device: no remote copies, remote signals or barrier semaphores. Data moves between devices by JAX's collectives and lax.ppermute only.
A program may use at most 128 MiB of HBM per device.

v0:
```python
import functools
import math

import jax
import jax.numpy as jnp
from jax import lax
from jax.experimental import pallas as pl
from jax.experimental.pallas import tpu as pltpu
from jax.sharding import PartitionSpec as P

F32 = jnp.float32
BF16 = jnp.bfloat16
EPSILON = 1e-05
HALO = 16
BLOCK = 128
VMEM_BYTES = 12 * 1024 * 1024


def call(body, outs, *args, scratch=(), flops=0, vmem=VMEM_BYTES):
    outs = [jax.ShapeDtypeStruct(shape, dtype) for shape, dtype in outs]
    moved = sum(a.size * a.dtype.itemsize for a in list(args[1:]) + outs)
    return pl.pallas_call(
        body,
        out_shape=outs,
        in_specs=[pl.BlockSpec(memory_space=pltpu.SMEM)]
        + [pl.BlockSpec(memory_space=pltpu.VMEM)] * (len(args) - 1),
        out_specs=[pl.BlockSpec(memory_space=pltpu.VMEM)] * len(outs),
        scratch_shapes=list(scratch),
        compiler_params=pltpu.CompilerParams(vmem_limit_bytes=vmem),
        cost_estimate=pl.CostEstimate(
            flops=int(flops), bytes_accessed=int(moved), transcendentals=0
        ),
    )(*args)


def dot(left, right):
    return jnp.dot(left, right, preferred_element_type=F32)


def dot_cols(left, right):
    return lax.dot_general(left, right, (((1,), (1,)), ((), ())), preferred_element_type=F32)


def dot_rows(left, right):
    return lax.dot_general(left, right, (((0,), (0,)), ((), ())), preferred_element_type=F32)


def normalized(stream):
    centred = stream - jnp.mean(stream, axis=1, keepdims=True)
    spread = lax.rsqrt(jnp.mean(centred * centred, axis=1, keepdims=True) + EPSILON)
    return centred * spread, spread


def norm_pullback(grad, stream, gain):
    normal, spread = normalized(stream)
    scaled = grad * gain
    first = jnp.mean(scaled, axis=1, keepdims=True)
    second = jnp.mean(scaled * normal, axis=1, keepdims=True)
    return spread * (scaled - first - normal * second), jnp.sum(
        grad * normal, axis=0, keepdims=True
    )


def swish_slope(value, logistic):
    return logistic * (1.0 + value * (1.0 - logistic))


def halves(idx, rows):
    half = rows // 2
    mine = pl.multiple_of(idx[1] * half, half)
    theirs = pl.multiple_of((1 - idx[1]) * half, half)
    return pl.ds(mine, half), pl.ds(theirs, half)


def split(idx, whole, keep, send):
    mine, theirs = halves(idx, whole.shape[0])
    keep[...] = whole[mine, :].astype(BF16)
    send[...] = whole[theirs, :].astype(BF16)


def join(idx, t_mine, t_theirs, whole):
    mine, theirs = halves(idx, whole.shape[0])
    whole[mine, :] = t_mine[...].astype(F32)
    whole[theirs, :] = t_theirs[...].astype(F32)


def xor_pairs(count, step):
    return [(i, i ^ step) for i in range(count)]


def swap(value, axis, step):
    return lax.ppermute(value, axis, xor_pairs(lax.axis_size(axis), step))


def added(left, right):
    return (left.astype(F32) + right.astype(F32)).astype(BF16)


def tp_sum(keep, send):
    count = lax.axis_size("tp")
    total = added(keep, swap(send, "tp", 1))
    step = 2
    while step < count:
        total = added(total, swap(total, "tp", step))
        step *= 2
    return total, swap(total, "tp", 1)


def place_body(ctx, later, idx, *refs):
    blocks = refs[: ctx + 2]
    out = refs[ctx + 2 + later]
    if later:
        refs[-1][...] = refs[ctx + 2][...]
    rows = blocks[0].shape[0]
    for at in range(2 * ctx):
        half = idx[2] if at < ctx else 1 - idx[2]
        target = half * ctx + jnp.bitwise_xor(idx[3], at % ctx)
        if at <= ctx:
            block = blocks[at][...]
        else:
            block = blocks[ctx + 1][(at - ctx - 1) * rows : (at - ctx) * rows, :]
        out[pl.ds(pl.multiple_of(target * rows, rows), rows), :] = block


def features_body(idx, *refs):
    blocks, gain_blocks = refs[:4], refs[4:8]
    x_out, cot_out, gains_out = refs[8:]
    rows, features = x_out.shape
    part = features // 4
    for at in range(4):
        target = jnp.bitwise_xor(idx[0], at)
        columns = pl.ds(pl.multiple_of(target * part, part), part)
        x_out[:, columns] = blocks[at][:rows, :]
        cot_out[:, columns] = blocks[at][rows:, :]
        gains_out[:, columns] = gain_blocks[at][...]


def wgrad_body(pairs, ordered, ctx, idx, *refs):
    out, scratch = refs[2 * pairs], refs[2 * pairs + 1]
    column = 0
    for at in range(pairs):
        left, right = refs[2 * at], refs[2 * at + 1]
        width = right.shape[1]
        product = dot_rows(left[...], right[...]).astype(BF16)
        if ordered:
            out[:, column : column + width] = product
        else:
            scratch[:, column : column + width] = product
        column += width
    if not ordered:
        rows = out.shape[0] // (2 * ctx)
        for at in range(2 * ctx):
            half = idx[2] if at < ctx else 1 - idx[2]
            source = half * ctx + jnp.bitwise_xor(idx[3], at % ctx)
            out[at * rows : (at + 1) * rows, :] = scratch[
                pl.ds(pl.multiple_of(source * rows, rows), rows), :
            ]


def feed_body(gain_at, base, joined, idx, *refs):
    if joined:
        x_ref, t1, t2, gains, weights, x_out, z_out, u_out, h_out, keep, send, work = refs
        join(idx, t1, t2, work)
        x = x_ref[...] + work[...]
        x_out[...] = x
    else:
        x_ref, gains, weights, z_out, u_out, h_out, keep, send, work = refs
        x = x_ref[...].astype(F32)
    hidden = u_out.shape[1]
    normal, unused = normalized(x)
    z = (normal * gains[gain_at : gain_at + 1, :]).astype(BF16)
    z_out[...] = z
    u = dot(z, weights[:, base : base + hidden])
    u_out[...] = u
    h = (u * jax.nn.sigmoid(u)).astype(BF16)
    h_out[...] = h
    work[...] = dot_cols(h, weights[:, base + hidden : base + 2 * hidden])
    split(idx, work, keep, send)


def attend_in_body(idx, x_ref, t1, t2, gains, weights, bias, x_out, z_out, qa, qb, kv, work):
    join(idx, t1, t2, work)
    x = x_ref[...].astype(F32) + 0.5 * work[...]
    x_out[...] = x
    normal, unused = normalized(x)
    z = (normal * gains[1:2, :]).astype(BF16)
    z_out[...] = z
    local = bias.shape[1]
    project = dot(z, weights[:, : 3 * local])
    query = project[:, :local]
    qa[...] = (query + bias[0:1, :]).astype(BF16)
    qb[...] = (query + bias[1:2, :]).astype(BF16)
    kv[...] = project[:, local:].astype(BF16)


def relative_body(base, idx, near_p, near_q, far_c, far_s, weights, embed, relative):
    step = far_c.shape[0]
    cos, sin = far_c[...], far_s[...]
    for at in range(embed.shape[0] // step):
        value = near_p[at : at + 1, :] * cos + near_q[at : at + 1, :] * sin
        embed[at * step : (at + 1) * step, :] = value.astype(BF16)
    relative[...] = dot(embed[...], weights[:, base : base + relative.shape[1]]).astype(BF16)


def position_body(heads, idx, qb, relative, out):
    rows, local = qb.shape
    size = local // heads
    length = out.shape[2]
    width = length + BLOCK
    for head in range(heads):
        columns = slice(head * size, (head + 1) * size)
        for at in range(rows // BLOCK):
            frames = slice(at * BLOCK, (at + 1) * BLOCK)
            first = rows - BLOCK * (at + 1)
            wide = dot_cols(qb[frames, columns], relative[first : first + width, columns])
            turned = pltpu.roll(wide, width - (BLOCK - 1), 1, stride=1, stride_axis=0)
            out[head, frames, :] = turned[:, :length]


def fill_pairs(idx, blocks, whole):
    rows = blocks[0].shape[0]
    for at, block in enumerate(blocks):
        target = jnp.bitwise_xor(idx[3], at)
        whole[pl.ds(pl.multiple_of(target * rows, rows), rows), :] = block[...]


def attend_body(heads, ctx, base, idx, qa, *refs):
    blocks = refs[:ctx]
    position, weights, p_out, mixed, keep, send, pairs, work = refs[ctx:]
    fill_pairs(idx, blocks, pairs)
    rows, local = qa.shape
    size = local // heads
    scale = size**-0.5
    for head in range(heads):
        columns = slice(head * size, (head + 1) * size)
        values = slice(local + head * size, local + (head + 1) * size)
        for at in range(rows // BLOCK):
            frames = slice(at * BLOCK, (at + 1) * BLOCK)
            scores = (dot_cols(qa[frames, columns], pairs[:, columns]) + position[head, frames, :]) * scale
            raised = jnp.exp(scores - jnp.max(scores, axis=1, keepdims=True))
            share = (raised / jnp.sum(raised, axis=1, keepdims=True)).astype(BF16)
            p_out[head, frames, :] = share
            mixed[frames, columns] = dot(share, pairs[:, values]).astype(BF16)
    work[...] = dot_cols(mixed[...], weights[:, base : base + local])
    split(idx, work, keep, send)


def conv_in_body(idx, x_ref, t1, t2, gains, weights, x_out, z_out, g_out, glu, first, last, work):
    join(idx, t1, t2, work)
    x = x_ref[...] + work[...]
    x_out[...] = x
    normal, unused = normalized(x)
    z = (normal * gains[2:3, :]).astype(BF16)
    z_out[...] = z
    rows, channels = glu.shape
    paired = dot(z, weights[:, : 2 * channels])
    g_out[...] = paired
    gated = (paired[:, :channels] * jax.nn.sigmoid(paired[:, channels:])).astype(BF16)
    glu[...] = gated
    first[...] = gated[:HALO, :]
    last[...] = gated[rows - HALO :, :]


def fill_padded(low, own, high, padded):
    rows = own.shape[0]
    padded[:HALO, :] = low[...].astype(F32)
    padded[HALO : HALO + rows, :] = own[...].astype(F32)
    padded[HALO + rows :, :] = high[...].astype(F32)


def conv_body(idx, glu, low, high, kernel, c_out, stats, padded):
    fill_padded(low, glu, high, padded)
    rows = glu.shape[0]
    taps = kernel.shape[0]
    shift = HALO - (taps - 1) // 2
    total = kernel[0:1, :] * padded[shift : shift + rows, :]
    for tap in range(1, taps):
        total = total + kernel[tap : tap + 1, :] * padded[shift + tap : shift + tap + rows, :]
    c_out[...] = total
    mean = jnp.mean(total, axis=0, keepdims=True)
    centred = total - mean
    stats[0:1, :] = mean
    stats[1:2, :] = jnp.sum(centred * centred, axis=0, keepdims=True)
    stats[2:, :] = jnp.zeros((stats.shape[0] - 2, stats.shape[1]), F32)


def batch_body(base, idx, c, stats, params, weights, q_out, act_out, keep, send, work):
    spread = stats[1:2, :]
    q = (c[...] - stats[0:1, :]) * spread
    q_out[...] = q
    a = q * params[0:1, :] + params[1:2, :]
    act = (a * jax.nn.sigmoid(a)).astype(BF16)
    act_out[...] = act
    work[...] = dot_cols(act, weights[:, base : base + act.shape[1]])
    split(idx, work, keep, send)


def feed_pullback(idx, grad, u, weights, base, f_out, du_out, keep, send, work):
    hidden = u.shape[1]
    f = (0.5 * grad).astype(BF16)
    f_out[...] = f
    value = u[...]
    logistic = jax.nn.sigmoid(value)
    back = dot(f, weights[:, base + hidden : base + 2 * hidden])
    du = (back * swish_slope(value, logistic)).astype(BF16)
    du_out[...] = du
    work[...] = dot_cols(du, weights[:, base : base + hidden])
    split(idx, work, keep, send)


def final_body(base, idx, x_ref, t1, t2, gains, cot, u, weights, y_out, d_out, gain_out, f_out, du_out, keep, send, work):
    join(idx, t1, t2, work)
    x = x_ref[...] + 0.5 * work[...]
    normal, unused = normalized(x)
    gain = gains[4:5, :]
    work[...] = normal * gain
    width = y_out.shape[1]
    y_out[...] = work[:, pl.ds(pl.multiple_of(idx[0] * width, width), width)].astype(BF16)
    grad, gain_grad = norm_pullback(cot[...].astype(F32), x, gain)
    gain_out[...] = gain_grad
    d_out[...] = grad
    feed_pullback(idx, grad, u, weights, base, f_out, du_out, keep, send, work)


def conv_back_body(base, idx, x_ref, d_ref, t1, t2, gains, q, params, weights, d_out, f_out, da_out, edges, gain_out, work):
    join(idx, t1, t2, work)
    grad, gain_grad = norm_pullback(work[...], x_ref[...], gains[3:4, :])
    gain_out[...] = gain_grad
    grad = d_ref[...] + grad
    d_out[...] = grad
    f = grad.astype(BF16)
    f_out[...] = f
    rows, channels = q.shape
    value = q[...]
    a = value * params[0:1, :] + params[1:2, :]
    da = dot(f, weights[:, base : base + channels]) * swish_slope(a, jax.nn.sigmoid(a))
    da_out[...] = da
    edges[0:1, :] = jnp.sum(da * value, axis=0, keepdims=True)
    edges[1:2, :] = jnp.sum(da, axis=0, keepdims=True)
    edges[2:8, :] = jnp.zeros((6, channels), F32)
    for at, part in enumerate((da[:HALO], value[:HALO], da[rows - HALO :], value[rows - HALO :])):
        edges[8 + at * HALO : 8 + (at + 1) * HALO, :] = part


def gate_back_body(ctx, counted, idx, da, q, own, near, far, stats, params, kernel, paired, weights, sums, dc_out, dg_out, keep, send, padded, work):
    rows, channels = q.shape
    sums[...] = own[:8, :] + far[:8, :]
    odd = idx[3] % 2 == 1
    low = jnp.where(odd, near[8 + 2 * HALO :, :], far[8 + 2 * HALO :, :])
    high = jnp.where(odd, far[8 : 8 + 2 * HALO, :], near[8 : 8 + 2 * HALO, :])
    factor = stats[1:2, :] * params[0:1, :]
    mean_scale = sums[0:1, :] / counted
    mean_shift = sums[1:2, :] / counted

    def centred(grad, normal):
        return (factor * (grad - mean_shift - normal * mean_scale)).astype(BF16)

    dc = centred(da[...], q[...])
    dc_out[...] = dc
    before = (idx[3] > 0).astype(F32)
    after = (idx[3] < ctx - 1).astype(F32)
    padded[:HALO, :] = centred(low[:HALO, :], low[HALO:, :]).astype(F32) * before
    padded[HALO : HALO + rows, :] = dc.astype(F32)
    padded[HALO + rows :, :] = centred(high[:HALO, :], high[HALO:, :]).astype(F32) * after
    taps = kernel.shape[0]
    top = HALO + (taps - 1) // 2
    total = kernel[0:1, :] * padded[top : top + rows, :]
    for tap in range(1, taps):
        total = total + kernel[tap : tap + 1, :] * padded[top - tap : top - tap + rows, :]
    logistic = jax.nn.sigmoid(paired[:, channels:])
    through = total * logistic
    dg_out[:, :channels] = through.astype(BF16)
    dg_out[:, channels:] = (through * paired[:, :channels] * (1.0 - logistic)).astype(BF16)
    work[...] = dot_cols(dg_out[...], weights[:, : 2 * channels])
    split(idx, work, keep, send)


def taps_body(idx, glu, low, high, dc, out, padded):
    fill_padded(low, glu, high, padded)
    rows = glu.shape[0]
    grad = dc[...].astype(F32)
    shift = HALO - (out.shape[0] - 1) // 2
    for tap in range(out.shape[0]):
        out[tap : tap + 1, :] = jnp.sum(
            grad * padded[shift + tap : shift + tap + rows, :], axis=0, keepdims=True
        )


def attend_back_body(heads, ctx, base, idx, x_ref, d_ref, t1, t2, gains, weights, p, qa, *refs):
    blocks = refs[:ctx]
    d_out, f_out, gain_out, ds_out, dqa = refs[ctx : ctx + 5]
    out_blocks = refs[ctx + 5 : 2 * ctx + 5]
    pairs, grads, do, work = refs[2 * ctx + 5 :]
    fill_pairs(idx, blocks, pairs)
    join(idx, t1, t2, work)
    grad, gain_grad = norm_pullback(work[...], x_ref[...], gains[2:3, :])
    gain_out[...] = gain_grad
    grad = d_ref[...] + grad
    d_out[...] = grad
    f = grad.astype(BF16)
    f_out[...] = f
    rows, local = qa.shape
    size = local // heads
    scale = size**-0.5
    do[...] = dot(f, weights[:, base : base + local]).astype(BF16)
    for head in range(heads):
        columns = slice(head * size, (head + 1) * size)
        values = slice(local + head * size, local + (head + 1) * size)
        for at in range(rows // BLOCK):
            frames = slice(at * BLOCK, (at + 1) * BLOCK)
            dp = dot_cols(do[frames, columns], pairs[:, values])
            share = p[head, frames, :].astype(F32)
            balance = jnp.sum(share * dp, axis=1, keepdims=True)
            ds = (share * (dp - balance)).astype(BF16)
            ds_out[head, frames, :] = ds
            dqa[frames, columns] = dot(ds, pairs[:, columns]) * scale
        grads[:, columns] = (dot_rows(ds_out[head], qa[:, columns]) * scale).astype(BF16)
        grads[:, values] = dot_rows(p[head], do[:, columns]).astype(BF16)
    for at, block in enumerate(out_blocks):
        source = jnp.bitwise_xor(idx[3], at)
        block[...] = grads[pl.ds(pl.multiple_of(source * rows, rows), rows), :]


def position_back_body(heads, idx, ds, qb, relative, dqb, dr_out, wide, total):
    rows, local = qb.shape
    size = local // heads
    length = ds.shape[2]
    width = length + BLOCK
    scale = size**-0.5
    down = lax.broadcasted_iota(jnp.int32, (BLOCK, BLOCK), 0)
    across = lax.broadcasted_iota(jnp.int32, (BLOCK, BLOCK), 1)
    flip = (down + across == BLOCK - 1).astype(BF16)
    total[...] = jnp.zeros(total.shape, F32)
    wide[:, length:] = jnp.zeros((BLOCK, BLOCK), F32)
    for head in range(heads):
        columns = slice(head * size, (head + 1) * size)
        for at in range(rows // BLOCK):
            frames = slice(at * BLOCK, (at + 1) * BLOCK)
            first = rows - BLOCK * (at + 1)
            wide[:, :length] = dot(flip, ds[head, frames, :])
            turned = pltpu.roll(wide[...], 0, 1, stride=1, stride_axis=0).astype(BF16)
            turned_b = dot(turned, relative[first : first + width, columns]) * scale
            dqb[frames, columns] = jnp.dot(
                flip.astype(F32), turned_b, precision=lax.Precision.HIGHEST, preferred_element_type=F32
            )
            flipped = dot(flip, qb[frames, columns]).astype(BF16)
            total[first : first + width, columns] += dot_rows(turned, flipped)
    dr_out[...] = (total[...] * scale).astype(BF16)


def attend_out_body(ctx, idx, dqa, dqb, *refs):
    blocks = refs[:ctx]
    weights, dp_out, bias_out, keep, send, work = refs[ctx:]
    local = dqa.shape[1]
    bias_out[0:1, :] = jnp.sum(dqa[...], axis=0, keepdims=True)
    bias_out[1:2, :] = jnp.sum(dqb[...], axis=0, keepdims=True)
    dp_out[:, :local] = (dqa[...] + dqb[...]).astype(BF16)
    total = blocks[0][...].astype(F32)
    for block in blocks[1:]:
        total = total + block[...].astype(F32)
    dp_out[:, local:] = total.astype(BF16)
    work[...] = dot_cols(dp_out[...], weights[:, : 3 * local])
    split(idx, work, keep, send)


def feed_back_body(idx, x_ref, d_ref, t1, t2, gains, u, x0, weights, d_out, f_out, du_out, gain_out, last_gain, keep, send, work):
    join(idx, t1, t2, work)
    grad, gain_grad = norm_pullback(work[...], x_ref[...], gains[1:2, :])
    gain_out[...] = gain_grad
    grad = d_ref[...] + grad
    d_out[...] = grad
    feed_pullback(idx, grad, u, weights, 0, f_out, du_out, keep, send, work)
    normal, unused = normalized(x0[...].astype(F32))
    last_gain[...] = jnp.sum(work[...] * normal, axis=0, keepdims=True)


def last_body(idx, x_ref, d_ref, t1, t2, gains, out, work):
    join(idx, t1, t2, work)
    grad, unused = norm_pullback(work[...], x_ref[...].astype(F32), gains[0:1, :])
    work[...] = d_ref[...] + grad
    width = out.shape[1]
    out[...] = work[:, pl.ds(pl.multiple_of(idx[0] * width, width), width)]


FRAMES = ("fsdp", "ctx")


def paired_mesh():
    return lax.axis_size("fsdp") == 2


def gathered(idx, shard, later=None):
    if not paired_mesh():
        whole = lax.all_gather(shard, FRAMES, axis=0, tiled=True)
        return whole if later is None else (whole, later)
    ctx = lax.axis_size("ctx")
    mine = [shard] + [swap(shard, "ctx", step) for step in range(1, ctx)]
    theirs = [swap(shard, "fsdp", 1), swap(jnp.concatenate(mine[1:], axis=0), "fsdp", 1)]
    rows, width = shard.shape
    outs = [((2 * ctx * rows, width), BF16)]
    handed = [] if later is None else [later]
    outs += [(later.shape, later.dtype)] if handed else []
    results = call(
        functools.partial(place_body, ctx, len(handed)), outs, idx, *mine, *theirs, *handed
    )
    return results if handed else results[0]


def features_whole(value):
    far = swap(value, "tp", 2)
    return [value, swap(value, "tp", 1), far, swap(far, "tp", 1)]


def weight_grads(idx, pairs, ordered):
    depth = pairs[0][0].shape[1]
    width = sum(right.shape[1] for unused, right in pairs)
    flat = [array for pair in pairs for array in pair]
    ctx = lax.axis_size("ctx")
    flops = sum(2 * left.shape[0] * depth * right.shape[1] for left, right in pairs)
    return call(
        functools.partial(wgrad_body, len(pairs), ordered, ctx),
        [((depth, width), BF16)],
        idx,
        *flat,
        scratch=[pltpu.VMEM((8, 128) if ordered else (depth, width), BF16)],
        flops=flops,
    )[0]


def scattered(idx, pairs, direct):
    direct = direct and paired_mesh()
    grads = weight_grads(idx, pairs, not direct)
    if not direct:
        return lax.psum_scatter(grads, FRAMES, scatter_dimension=0, tiled=True).astype(F32)
    ctx = lax.axis_size("ctx")
    half = grads.shape[0] // 2
    rows = half // ctx
    total = added(grads[:half], swap(grads[half:], "fsdp", 1))
    parts = [total[:rows]]
    for step in range(1, ctx):
        parts.append(swap(total[step * rows : (step + 1) * rows], "ctx", step))
    return sum(part.astype(F32) for part in parts)


def over_frames(value, merge):
    for axis in ("fsdp", "ctx"):
        step = 1
        while step < lax.axis_size(axis):
            value = merge(value, swap(value, axis, step))
            step *= 2
    return value


def summed(value):
    return over_frames(value, lambda left, right: left + right)


def pooled(stats, rows):
    count = [rows]

    def merge(left, right):
        gap = left[0:1] - right[0:1]
        mean = 0.5 * (left[0:1] + right[0:1])
        squares = left[1:2] + right[1:2] + gap * gap * (0.5 * count[0])
        count[0] *= 2
        return jnp.concatenate([mean, squares, left[2:]], axis=0)

    stats = over_frames(stats, merge)
    spread = lax.rsqrt(stats[1:2] / count[0] + EPSILON)
    return jnp.concatenate([stats[0:1], spread, stats[2:]], axis=0)


def edges_summed(edges):
    step = 1
    while step < lax.axis_size("fsdp"):
        edges = jnp.concatenate([edges[:8] + swap(edges[:8], "fsdp", step), edges[8:]], axis=0)
        step *= 2
    near = swap(edges, "ctx", 1)
    own = jnp.concatenate([edges[:8] + near[:8], edges[8:]], axis=0)
    return own, near, swap(own, "ctx", 3)


def neighbours(first, last):
    count = lax.axis_size("ctx")
    up = [(i, i + 1) for i in range(count - 1)]
    down = [(i + 1, i) for i in range(count - 1)]
    return lax.ppermute(last, "ctx", up), lax.ppermute(first, "ctx", down)


def angle_tables(start, rows, width, features):
    step = 64
    column = jnp.arange(features, dtype=jnp.int32)
    rates = jnp.exp((column // 2).astype(F32) * (-2.0 * math.log(10000.0) / features))
    even = (column % 2 == 0)[None, :]
    near = (start + rows - 1 - step * jnp.arange(width // step, dtype=jnp.int32)).astype(F32)
    near = near[:, None] * rates[None, :]
    far = jnp.arange(step, dtype=jnp.int32).astype(F32)[:, None] * rates[None, :]
    sine, cosine = jnp.sin(near), jnp.cos(near)
    return (
        jnp.where(even, sine, cosine),
        jnp.where(even, -cosine, sine),
        jnp.cos(far),
        jnp.sin(far),
    )


def shards(
    tokens,
    first_expand,
    first_shrink,
    attend_input,
    position_map,
    position_bias,
    attend_output,
    gating_map,
    depth_kernel,
    batch_scale,
    batch_shift,
    mixing_map,
    second_expand,
    second_shrink,
    layer_gains,
    cotangent,
):
    rows, part = tokens.shape
    tp, ctx = lax.axis_size("tp"), lax.axis_size("ctx")
    features = part * tp
    shard = first_expand.shape[0]
    hidden = first_expand.shape[1]
    heads, size = position_bias.shape[1:]
    local = heads * size
    channels = depth_kernel.shape[1]
    length = rows * ctx
    width = length + rows
    tp_at = lax.axis_index("tp")
    ctx_at = lax.axis_index("ctx")
    idx = jnp.stack(
        [tp_at, tp_at % 2, lax.axis_index("fsdp"), ctx_at]
    ).astype(jnp.int32)

    last_shard = jnp.concatenate(
        [
            gating_map.reshape(shard, 2 * channels),
            mixing_map.T,
            second_expand,
            second_shrink.T,
        ],
        axis=1,
    )
    one, last_shard = gathered(
        idx, jnp.concatenate([first_expand, first_shrink.T], axis=1), last_shard
    )
    x0, cot, gains = call(
        features_body,
        [((rows, features), BF16), ((rows, features), BF16), ((5, features), F32)],
        idx,
        *features_whole(jnp.concatenate([tokens, cotangent], axis=0)),
        *features_whole(layer_gains),
    )
    bias = position_bias.reshape(2, local)
    params = jnp.stack([batch_scale, batch_shift])
    tables = angle_tables(ctx_at * rows, rows, width, features)
    two = gathered(
        idx,
        jnp.concatenate(
            [attend_input.reshape(shard, 3 * local), position_map, attend_output.T], axis=1
        ),
    )
    three = lax.all_gather(last_shard, FRAMES, axis=0, tiled=True)
    at_pos, at_out = 3 * local, 4 * local
    at_mix, at_two = 2 * channels, 3 * channels

    stream = ((rows, features), F32)
    packed = ((rows, features), BF16)
    piece = ((rows // 2, features), BF16)
    gain_row = ((1, features), F32)
    work = pltpu.VMEM((rows, features), F32)
    feed_flops = 4 * rows * features * hidden

    feed_outs = [packed, ((rows, hidden), F32), ((rows, hidden), BF16), piece, piece]
    z1, u1, h1, keep, send = call(
        functools.partial(feed_body, 0, 0, False),
        feed_outs,
        idx,
        x0,
        gains,
        one,
        scratch=[work],
        flops=feed_flops,
    )
    t1, t2 = tp_sum(keep, send)
    embed, relative = call(
        functools.partial(relative_body, at_pos),
        [((width, features), BF16), ((width, local), BF16)],
        idx,
        *tables,
        two,
        flops=2 * width * features * local,
    )
    per_head = ((rows, local), BF16)
    x1, z2, qa, qb, kv = call(
        attend_in_body,
        [stream, packed, per_head, per_head, ((rows, 2 * local), BF16)],
        idx,
        x0,
        t1,
        t2,
        gains,
        two,
        bias,
        scratch=[work],
        flops=6 * rows * features * local,
    )
    pairs = [kv] + [swap(kv, "ctx", step) for step in range(1, ctx)]
    position = call(
        functools.partial(position_body, heads),
        [((heads, rows, length), F32)],
        idx,
        qb,
        relative,
        flops=2 * rows * (length + BLOCK) * local * 8,
    )[0]
    whole_pairs = pltpu.VMEM((length, 2 * local), BF16)
    p, mixed, keep, send = call(
        functools.partial(attend_body, heads, ctx, at_out),
        [((heads, rows, length), BF16), per_head, piece, piece],
        idx,
        qa,
        *pairs,
        position,
        two,
        scratch=[whole_pairs, work],
        flops=4 * rows * length * local * 8,
    )
    t1, t2 = tp_sum(keep, send)
    edge = ((HALO, channels), BF16)
    x2, z3, paired, glu, first, last = call(
        conv_in_body,
        [stream, packed, ((rows, 2 * channels), F32), ((rows, channels), BF16), edge, edge],
        idx,
        x1,
        t1,
        t2,
        gains,
        three,
        scratch=[work],
        flops=4 * rows * features * channels,
    )
    low, high = neighbours(first, last)
    padded = pltpu.VMEM((rows + 2 * HALO, channels), F32)
    c, stats = call(
        conv_body,
        [((rows, channels), F32), ((8, channels), F32)],
        idx,
        glu,
        low,
        high,
        depth_kernel,
        scratch=[padded],
    )
    stats = pooled(stats, rows)
    q, act, keep, send = call(
        functools.partial(batch_body, at_mix),
        [((rows, channels), F32), ((rows, channels), BF16), piece, piece],
        idx,
        c,
        stats,
        params,
        three,
        scratch=[work],
        flops=2 * rows * features * channels,
    )
    t1, t2 = tp_sum(keep, send)
    x3, z4, u2, h2, keep, send = call(
        functools.partial(feed_body, 3, at_two, True),
        [stream] + feed_outs,
        idx,
        x2,
        t1,
        t2,
        gains,
        three,
        scratch=[work],
        flops=feed_flops,
    )
    t1, t2 = tp_sum(keep, send)
    outputs, d4, gain_five, f4, du2, keep, send = call(
        functools.partial(final_body, at_two),
        [((rows, part), BF16), stream, gain_row, packed, ((rows, hidden), BF16), piece, piece],
        idx,
        x3,
        t1,
        t2,
        gains,
        cot,
        u2,
        three,
        scratch=[work],
        flops=feed_flops,
    )
    t1, t2 = tp_sum(keep, send)
    d3, f3, da, edges, gain_four = call(
        functools.partial(conv_back_body, at_mix),
        [stream, packed, ((rows, channels), F32), ((8 + 4 * HALO, channels), F32), gain_row],
        idx,
        x3,
        d4,
        t1,
        t2,
        gains,
        q,
        params,
        three,
        scratch=[work],
        flops=2 * rows * features * channels,
    )
    own, near, far = edges_summed(edges)
    counted = rows * lax.axis_size(FRAMES)
    sums, dc, dg, keep, send = call(
        functools.partial(gate_back_body, ctx, counted),
        [((8, channels), F32), ((rows, channels), BF16), ((rows, 2 * channels), BF16), piece, piece],
        idx,
        da,
        q,
        own,
        near,
        far,
        stats,
        params,
        depth_kernel,
        paired,
        three,
        scratch=[padded, work],
        flops=4 * rows * features * channels,
    )
    t1, t2 = tp_sum(keep, send)
    kernel_grad = call(
        taps_body,
        [(depth_kernel.shape, F32)],
        idx,
        glu,
        low,
        high,
        dc,
        scratch=[padded],
    )[0]
    middle = scattered(idx, [(z3, dg), (f3, act), (z4, du2), (f4, h2)], False)
    pair_block = ((rows, 2 * local), BF16)
    results = call(
        functools.partial(attend_back_body, heads, ctx, at_out),
        [stream, packed, gain_row, ((heads, rows, length), BF16), ((rows, local), F32)]
        + [pair_block] * ctx,
        idx,
        x2,
        d3,
        t1,
        t2,
        gains,
        two,
        p,
        qa,
        *pairs,
        scratch=[whole_pairs, whole_pairs, pltpu.VMEM((rows, local), BF16), work],
        flops=8 * rows * length * local * 4,
    )
    d2, f2, gain_three, ds, dqa = results[:5]
    pair_grads = [results[5]] + [
        swap(block, "ctx", step + 1) for step, block in enumerate(results[6:])
    ]
    dqb, dr = call(
        functools.partial(position_back_body, heads),
        [((rows, local), F32), ((width, local), BF16)],
        idx,
        ds,
        qb,
        relative,
        scratch=[pltpu.VMEM((BLOCK, length + BLOCK), F32), pltpu.VMEM((width, local), F32)],
        flops=4 * rows * (length + BLOCK) * local * 8,
    )
    dp, bias_grad, keep, send = call(
        functools.partial(attend_out_body, ctx),
        [((rows, 3 * local), BF16), ((2, local), F32), piece, piece],
        idx,
        dqa,
        dqb,
        *pair_grads,
        two,
        scratch=[work],
        flops=6 * rows * features * local,
    )
    t1, t2 = tp_sum(keep, send)
    inner = scattered(idx, [(z2, dp), (embed, dr), (f2, mixed)], True)
    d1, f1, du1, gain_two, gain_one, keep, send = call(
        feed_back_body,
        [stream, packed, ((rows, hidden), BF16), gain_row, gain_row, piece, piece],
        idx,
        x1,
        d2,
        t1,
        t2,
        gains,
        u1,
        x0,
        one,
        scratch=[work],
        flops=feed_flops,
    )
    t1, t2 = tp_sum(keep, send)
    front_b = scattered(idx, [(f1, h1)], True)
    front_a = scattered(idx, [(z1, du1)], True)
    step = 1
    while step < tp:
        gain_one = gain_one + swap(gain_one, "tp", step)
        step *= 2
    rows_grad = lax.dynamic_slice_in_dim(
        jnp.concatenate([gain_one, gain_two, gain_three, gain_four, gain_five], axis=0),
        tp_at * part,
        part,
        axis=1,
    )
    small = summed(jnp.concatenate([rows_grad, bias_grad, kernel_grad], axis=0))
    taps = depth_kernel.shape[0]
    tokens_grad = call(
        last_body,
        [((rows, part), F32)],
        idx,
        x0,
        d1,
        t1,
        t2,
        gains,
        scratch=[work],
    )[0]
    return (
        outputs,
        tokens_grad,
        front_a,
        front_b.T,
        inner[:, :at_pos].reshape(shard, 3, local),
        inner[:, at_pos:at_out],
        small[5:7].reshape(2, heads, size),
        inner[:, at_out:].T,
        middle[:, :at_mix].reshape(shard, 2, channels),
        small[7 : 7 + taps],
        sums[0],
        sums[1],
        middle[:, at_mix:at_two].T,
        middle[:, at_two : at_two + hidden],
        middle[:, at_two + hidden :].T,
        small[:5],
    )


def solution(mesh):
    frames = ("fsdp", "ctx")
    rows, columns = P(frames, "tp"), P("tp", frames)
    three_dims, last_only, one_dim = P(frames, None, "tp"), P(None, "tp"), P("tp")
    heads = P(None, "tp", None)
    return jax.shard_map(
        shards,
        mesh=mesh,
        in_specs=(
            rows,
            rows,
            columns,
            three_dims,
            rows,
            heads,
            columns,
            three_dims,
            last_only,
            one_dim,
            one_dim,
            columns,
            rows,
            columns,
            last_only,
            rows,
        ),
        out_specs=(
            rows,
            rows,
            rows,
            columns,
            three_dims,
            rows,
            heads,
            columns,
            three_dims,
            last_only,
            one_dim,
            one_dim,
            columns,
            rows,
            columns,
            last_only,
        ),
        check_vma=False,
    )
```

profile of v0, /device:TPU:0, one launch (start us, length us, event | category | flops | bytes accessed | tf_op | source)
XLA Modules:
  0.0 318.7 jit_solution(13424517385968754845)
XLA Ops:
  7.8 2.6 collective-permute-start.4
  11.2 3.7 %collective-permute-start.8 = (bf16[64,1024]{1,0:T(8,128)(2,1)S(1)}, bf16[64,1024]{1,0:T(8,128)(2,1)S(1)}, u32[]{:S(2)}, u32[]{:S(2)}) collective-permute-start(bf16[64,1024]{1,0:T(8,128)(2,1)S(1)} %pad_maximum_fusion.3.refs_0_), channel_id=1, source_target_pairs={{0,12},{4,8},{8,4},{12,0},{1,13},{5,9},{9,5},{13,1},{2,14},{6,10},... | collective-permute-start | bytes 393224 | tf_op jit(solution)/shard_map/ppermute | solution.py:92
  19.5 1.5 collective-permute-start.9
  21.0 5.3 %collective-permute-done.7.refs_2_ = bf16[64,1024]{1,0:T(8,128)(2,1)S(1)} collective-permute-done((bf16[64,1024]{1,0:T(8,128)(2,1)S(1)}, bf16[64,1024]{1,0:T(8,128)(2,1)S(1)}, u32[]{:S(2)}, u32[]{:S(2)}) %collective-permute-start.7) | collective-permute-done | bytes 131104 | tf_op jit(solution)/shard_map/ppermute | solution.py:92
  26.9 1.6 collective-permute-start.10
  28.5 3.9 %collective-permute-done.1.refs_2_ = bf16[768,128]{1,0:T(8,128)(2,1)S(1)} collective-permute-done((bf16[768,128]{1,0:T(8,128)(2,1)S(1)}, bf16[768,128]{1,0:T(8,128)(2,1)S(1)}, u32[]{:S(2)}, u32[]{:S(2)}) %collective-permute-start.1) | collective-permute-done | bytes 196640 | tf_op jit(solution)/shard_map/ppermute | solution.py:92
  34.6 1.5 collective-permute-start.17
  36.1 2.5 collective-permute-start.16
  40.7 1.9 collective-permute-start.14
  44.2 1.5 shard_map.281
  49.0 1.7 add_convert_fusion.18
  52.4 5.5 %collective-permute-done.12 = bf16[192,512]{1,0:T(8,128)(2,1)} collective-permute-done((bf16[192,512]{1,0:T(8,128)(2,1)}, bf16[192,512]{1,0:T(8,128)(2,1)}, u32[]{:S(2)}, u32[]{:S(2)}) %collective-permute-start.12) | collective-permute-done | bytes 196640 | tf_op jit(solution)/shard_map/ppermute | solution.py:92
  59.1 2.4 collective-permute-done.18.refs_5_
  65.4 2.5 collective-permute-start.21
  67.8 1.9 collective-permute-start.19
  72.7 3.1 shard_map.285.refs_4_
  75.9 14.9 %collective-permute-done.20.refs_2_ = bf16[384,256]{1,0:T(8,128)(2,1)S(1)} collective-permute-done((bf16[384,256]{1,0:T(8,128)(2,1)S(1)}, bf16[384,256]{1,0:T(8,128)(2,1)S(1)}, u32[]{:S(2)}, u32[]{:S(2)}) %collective-permute-start.20) | collective-permute-done | bytes 196640 | tf_op jit(solution)/shard_map/ppermute | solution.py:92
  90.8 4.6 %shard_map.286 = (bf16[2,384,1536]{2,1,0:T(8,128)(2,1)S(1)}, bf16[384,128]{1,0:T(8,128)(2,1)S(1)}, bf16[192,512]{1,0:T(8,128)(2,1)S(1)}, bf16[192,512]{1,0:T(8,128)(2,1)S(1)}) custom-call(s32[4]{0:T(128)S(1)} %pad_add_fusion.idx, bf16[384,128]{1,0:T(8,128)(2,1)S(1)} %get-tuple-element.100.qa, bf16[384,256]{1,0:T(8,128)(2,1)S(1)} %get-tuple-element.101.refs_0_, ...), custom_call_target="tpu_custom_call" | custom-call | flops 2415919104 | bytes 9109504 | tf_op jit(solution)/shard_map/pallas_call | solution.py:22
  98.4 1.4 collective-permute-start.23
  99.9 5.6 %collective-permute-done.23 = bf16[192,512]{1,0:T(8,128)(2,1)S(1)} collective-permute-done((bf16[192,512]{1,0:T(8,128)(2,1)S(1)}, bf16[192,512]{1,0:T(8,128)(2,1)S(1)}, u32[]{:S(2)}, u32[]{:S(2)}) %collective-permute-start.23) | collective-permute-done | bytes 196640 | tf_op jit(solution)/shard_map/ppermute | solution.py:92
  110.2 1.7 collective-permute-start.25
  111.9 1.5 collective-permute-start.26
  113.4 4.0 %collective-permute-done.26.high = bf16[16,128]{1,0:T(8,128)(2,1)S(1)} collective-permute-done((bf16[16,128]{1,0:T(8,128)(2,1)S(1)}, bf16[16,128]{1,0:T(8,128)(2,1)S(1)}, u32[]{:S(2)}, u32[]{:S(2)}) %collective-permute-start.26) | collective-permute-done | bytes 4128 | tf_op jit(solution)/shard_map/ppermute | solution.py:587
  118.8 3.6 %collective-permute-done.27 = f32[8,128]{1,0:T(8,128)S(1)} collective-permute-done((f32[8,128]{1,0:T(8,128)S(1)}, f32[8,128]{1,0:T(8,128)S(1)}, u32[]{:S(2)}, u32[]{:S(2)}) %collective-permute-start.27) | collective-permute-done | bytes 4128 | tf_op jit(solution)/shard_map/ppermute | solution.py:92
  122.4 2.3 collective-permute-start.28
  124.6 1.6 collective-permute-done.28
  126.2 3.5 %collective-permute-start.29 = (f32[8,128]{1,0:T(8,128)S(1)}, f32[8,128]{1,0:T(8,128)S(1)}, u32[]{:S(2)}, u32[]{:S(2)}) collective-permute-start(f32[8,128]{1,0:T(8,128)S(1)} %maximum_maximum_fusion.1), channel_id=1, source_target_pairs={{0,8},{4,12},{8,0},{12,4},{1,9},{5,13},{9,1},{13,5},{2,10},{6,14},... | collective-permute-start | bytes 12296 | tf_op jit(solution)/shard_map/ppermute | solution.py:92
  129.8 1.6 collective-permute-done.29
  132.9 1.4 collective-permute-done.30
  135.7 5.7 %collective-permute-done.31 = bf16[192,512]{1,0:T(8,128)(2,1)S(1)} collective-permute-done((bf16[192,512]{1,0:T(8,128)(2,1)S(1)}, bf16[192,512]{1,0:T(8,128)(2,1)S(1)}, u32[]{:S(2)}, u32[]{:S(2)}) %collective-permute-start.31) | collective-permute-done | bytes 196640 | tf_op jit(solution)/shard_map/ppermute | solution.py:92
  143.0 1.6 shard_map.290
  147.4 5.7 %collective-permute-done.34 = bf16[192,512]{1,0:T(8,128)(2,1)S(1)} collective-permute-done((bf16[192,512]{1,0:T(8,128)(2,1)S(1)}, bf16[192,512]{1,0:T(8,128)(2,1)S(1)}, u32[]{:S(2)}, u32[]{:S(2)}) %collective-permute-start.34) | collective-permute-done | bytes 196640 | tf_op jit(solution)/shard_map/ppermute | solution.py:92
  154.7 2.3 shard_map.291
  159.8 5.7 %collective-permute-done.37 = bf16[192,512]{1,0:T(8,128)(2,1)S(1)} collective-permute-done((bf16[192,512]{1,0:T(8,128)(2,1)S(1)}, bf16[192,512]{1,0:T(8,128)(2,1)S(1)}, u32[]{:S(2)}, u32[]{:S(2)}) %collective-permute-start.37) | collective-permute-done | bytes 196640 | tf_op jit(solution)/shard_map/ppermute | solution.py:92
  168.6 3.6 %collective-permute-done.39 = f32[8,128]{1,0:T(8,128)S(1)} collective-permute-done((f32[8,128]{1,0:T(8,128)S(1)}, f32[8,128]{1,0:T(8,128)S(1)}, u32[]{:S(2)}, u32[]{:S(2)}) %collective-permute-start.39) | collective-permute-done | bytes 4128 | tf_op jit(solution)/shard_map/ppermute | solution.py:92
  172.2 1.5 collective-permute-start.40
  173.7 2.5 collective-permute-done.40.near
  176.2 2.4 collective-permute-start.41
  178.6 3.4 %collective-permute-done.41.far = f32[72,128]{1,0:T(8,128)S(1)} collective-permute-done((f32[72,128]{1,0:T(8,128)S(1)}, f32[72,128]{1,0:T(8,128)S(1)}, u32[]{:S(2)}, u32[]{:S(2)}) %collective-permute-start.41) | collective-permute-done | bytes 36896 | tf_op jit(solution)/shard_map/ppermute | solution.py:92
  186.3 5.7 %collective-permute-done.43 = bf16[192,512]{1,0:T(8,128)(2,1)S(1)} collective-permute-done((bf16[192,512]{1,0:T(8,128)(2,1)S(1)}, bf16[192,512]{1,0:T(8,128)(2,1)S(1)}, u32[]{:S(2)}, u32[]{:S(2)}) %collective-permute-start.43) | collective-permute-done | bytes 196640 | tf_op jit(solution)/shard_map/ppermute | solution.py:92
  193.7 5.9 %shard_map.294 = (f32[384,512]{1,0:T(8,128)S(1)}, bf16[384,512]{1,0:T(8,128)(2,1)S(1)}, f32[1,512]{1,0:T(1,128)S(1)}, bf16[2,384,1536]{2,1,0:T(8,128)(2,1)S(1)},...) custom-call(s32[4]{0:T(128)S(1)} %pad_add_fusion.idx, ...), custom_call_target="tpu_custom_call" | custom-call | flops 2415919104 | bytes 10399744 | tf_op jit(solution)/shard_map/pallas_call | solution.py:22
  199.7 3.0 collective-permute-start.46
  204.1 5.5 %shard_map.295 = (f32[384,128]{1,0:T(8,128)S(1)}, bf16[1920,128]{1,0:T(8,128)(2,1)S(1)}) custom-call(s32[4]{0:T(128)S(1)} %pad_add_fusion.idx, bf16[2,384,1536]{2,1,0:T(8,128)(2,1)S(1)} %get-tuple-element.134.ds, bf16[384,128]{1,0:T(8,128)(2,1)S(1)} %copy-done.56, bf16[1920,128]{1,0:T(8,128)(2,1)S(1)} %copy-done.12), custom_call_target="tpu_custom_call" | custom-call | flops 2617245696 | bytes 3637248 | tf_op jit(solution)/shard_map/pallas_call | solution.py:22
  210.5 6.5 %collective-permute-done.46.refs_2_ = bf16[384,256]{1,0:T(8,128)(2,1)S(1)} collective-permute-done((bf16[384,256]{1,0:T(8,128)(2,1)S(1)}, bf16[384,256]{1,0:T(8,128)(2,1)S(1)}, u32[]{:S(2)}, u32[]{:S(2)}) %collective-permute-start.46) | collective-permute-done | bytes 196640 | tf_op jit(solution)/shard_map/ppermute | solution.py:92
  218.7 1.4 collective-permute-done.48
  229.9 2.7 shard_map.303
  234.2 1.5 copy-done.4
  239.6 1.7 shard_map.301
  244.0 1.9 shard_map.297
  248.6 3.3 %collective-permute-done.62 = bf16[256,640]{1,0:T(8,128)(2,1)S(1)} collective-permute-done((bf16[256,640]{1,0:T(8,128)(2,1)S(1)}, bf16[256,640]{1,0:T(8,128)(2,1)S(1)}, u32[]{:S(2)}, u32[]{:S(2)}) %collective-permute-start.62) | collective-permute-done | bytes 327712 | tf_op jit(solution)/shard_map/ppermute | solution.py:92
  252.1 1.5 collective-permute-start.67
  253.7 2.3 collective-permute-start.63
  255.9 2.9 collective-permute-start.65
  260.6 5.4 %collective-permute-done.65 = bf16[64,640]{1,0:T(8,128)(2,1)S(1)} collective-permute-done((bf16[64,640]{1,0:T(8,128)(2,1)S(1)}, bf16[64,640]{1,0:T(8,128)(2,1)S(1)}, u32[]{:S(2)}, u32[]{:S(2)}) %collective-permute-start.65) | collective-permute-done | bytes 81952 | tf_op jit(solution)/shard_map/ppermute | solution.py:92
  266.0 2.4 collective-permute-done.64
  272.9 1.9 collective-permute-start.70
  283.6 1.8 collective-permute-start.57
  287.4 2.1 collective-permute-start.59
  289.5 2.4 collective-permute-start.61
  293.3 4.7 %collective-permute-done.61 = bf16[64,512]{1,0:T(8,128)(2,1)S(1)} collective-permute-done((bf16[64,512]{1,0:T(8,128)(2,1)S(1)}, bf16[64,512]{1,0:T(8,128)(2,1)S(1)}, u32[]{:S(2)}, u32[]{:S(2)}) %collective-permute-start.61) | collective-permute-done | bytes 65568 | tf_op jit(solution)/shard_map/ppermute | solution.py:92
  298.1 3.3 %collective-permute-done.60 = bf16[64,512]{1,0:T(8,128)(2,1)S(1)} collective-permute-done((bf16[64,512]{1,0:T(8,128)(2,1)S(1)}, bf16[64,512]{1,0:T(8,128)(2,1)S(1)}, u32[]{:S(2)}, u32[]{:S(2)}) %collective-permute-start.60) | collective-permute-done | bytes 65568 | tf_op jit(solution)/shard_map/ppermute | solution.py:92
  302.1 1.8 shard_map.298
  303.9 2.4 reduce-scatter.2.cloned.1.call-done
  310.0 1.5 slice.199
  (357 shorter events, 102.5 us)
Async XLA Ops:
  7.2 99.8 %all-gather.2.cloned.1.call-start = ((), (), s32[]{:S(2)}) async-start(), calls=%async_computation.1 | async-start | bytes 1622016 | tf_op jit(solution)/shard_map/all_gather | solution.py:669
  7.2 21.2 %collective-permute-start.3 = (f32[5,128]{1,0:T(8,128)}, f32[5,128]{1,0:T(8,128)S(1)}, u32[]{:S(2)}, u32[]{:S(2)}) collective-permute-start(f32[5,128]{1,0:T(8,128)} %refs_4_.1), channel_id=1, source_target_pairs={{0,1},{1,0},{2,3},{3,2},{4,5},{5,4},{6,7},{7,6},{8,9},{9,8},{10,11... | collective-permute-start | bytes 7688 | tf_op jit(solution)/shard_map/ppermute | solution.py:92
  7.8 25.5 %collective-permute-start.4 = (f32[5,128]{1,0:T(8,128)}, f32[5,128]{1,0:T(8,128)S(1)}, u32[]{:S(2)}, u32[]{:S(2)}) collective-permute-start(f32[5,128]{1,0:T(8,128)} %refs_4_.1), channel_id=1, source_target_pairs={{0,2},{1,3},{2,0},{3,1},{4,6},{5,7},{6,4},{7,5},{8,10},{9,11},{10,... | collective-permute-start | bytes 7688 | tf_op jit(solution)/shard_map/ppermute | solution.py:92
  11.2 8.3 %collective-permute-start.8 = (bf16[64,1024]{1,0:T(8,128)(2,1)S(1)}, bf16[64,1024]{1,0:T(8,128)(2,1)S(1)}, u32[]{:S(2)}, u32[]{:S(2)}) collective-permute-start(bf16[64,1024]{1,0:T(8,128)(2,1)S(1)} %pad_maximum_fusion.3.refs_0_), channel_id=1, source_target_pairs={{0,12},{4,8},{8,4},{12,0},{1,13},{5,9},{9,5},{13,1},{2,14},{6,10},... | collective-permute-start | bytes 393224 | tf_op jit(solution)/shard_map/ppermute | solution.py:92
  14.9 11.4 %collective-permute-start.7 = (bf16[64,1024]{1,0:T(8,128)(2,1)S(1)}, bf16[64,1024]{1,0:T(8,128)(2,1)S(1)}, u32[]{:S(2)}, u32[]{:S(2)}) collective-permute-start(bf16[64,1024]{1,0:T(8,128)(2,1)S(1)} %pad_maximum_fusion.3.refs_0_), channel_id=1, source_target_pairs={{0,8},{4,12},{8,0},{12,4},{1,9},{5,13},{9,1},{13,5},{2,10},{6,14},... | collective-permute-start | bytes 393224 | tf_op jit(solution)/shard_map/ppermute | solution.py:92
  14.9 11.9 %collective-permute-start.6 = (bf16[64,1024]{1,0:T(8,128)(2,1)S(1)}, bf16[64,1024]{1,0:T(8,128)(2,1)S(1)}, u32[]{:S(2)}, u32[]{:S(2)}) collective-permute-start(bf16[64,1024]{1,0:T(8,128)(2,1)S(1)} %pad_maximum_fusion.3.refs_0_), channel_id=1, source_target_pairs={{0,4},{4,0},{8,12},{12,8},{1,5},{5,1},{9,13},{13,9},{2,6},{6,2},{1... | collective-permute-start | bytes 393224 | tf_op jit(solution)/shard_map/ppermute | solution.py:92
  19.5 20.5 %collective-permute-start.9 = (bf16[64,1024]{1,0:T(8,128)(2,1)S(1)}, bf16[64,1024]{1,0:T(8,128)(2,1)S(1)}, u32[]{:S(2)}, u32[]{:S(2)}) collective-permute-start(bf16[64,1024]{1,0:T(8,128)(2,1)S(1)} %pad_maximum_fusion.3.refs_0_), channel_id=1, source_target_pairs={{0,16},{16,0},{1,17},{17,1},{2,18},{18,2},{3,19},{19,3},{4,20},{20... | collective-permute-start | bytes 393224 | tf_op jit(solution)/shard_map/ppermute | solution.py:92
  26.3 6.1 %collective-permute-start.1 = (bf16[768,128]{1,0:T(8,128)(2,1)S(1)}, bf16[768,128]{1,0:T(8,128)(2,1)S(1)}, u32[]{:S(2)}, u32[]{:S(2)}) collective-permute-start(bf16[768,128]{1,0:T(8,128)(2,1)S(1)} %constant_dynamic-update-slice_fusion.refs_0_), channel_id=1, source_target_pairs={{0,2},{1,3},{2,0},{3,1},{4,6},{5,7},{6,4},{7,5},{8,10},{9,11},{10,... | collective-permute-start | bytes 589832 | tf_op jit(solution)/shard_map/ppermute | solution.py:92
  26.9 15.8 %collective-permute-start.10 = (bf16[192,1024]{1,0:T(8,128)(2,1)S(1)}, bf16[192,1024]{1,0:T(8,128)(2,1)S(1)}, u32[]{:S(2)}, u32[]{:S(2)}) collective-permute-start(bf16[192,1024]{1,0:T(8,128)(2,1)S(1)} %pad_maximum_fusion), channel_id=1, source_target_pairs={{0,16},{16,0},{1,17},{17,1},{2,18},{18,2},{3,19},{19,3},{4,20},{20... | collective-permute-start | bytes 1179656 | tf_op jit(solution)/shard_map/ppermute | solution.py:92
  28.4 7.7 %collective-permute-start = (bf16[768,128]{1,0:T(8,128)(2,1)S(1)}, bf16[768,128]{1,0:T(8,128)(2,1)S(1)}, u32[]{:S(2)}, u32[]{:S(2)}) collective-permute-start(bf16[768,128]{1,0:T(8,128)(2,1)S(1)} %constant_dynamic-update-slice_fusion.refs_0_), channel_id=1, source_target_pairs={{0,1},{1,0},{2,3},{3,2},{4,5},{5,4},{6,7},{7,6},{8,9},{9,8},{10,11... | collective-permute-start | bytes 589832 | tf_op jit(solution)/shard_map/ppermute | solution.py:92
  32.5 6.2 %collective-permute-start.2 = (bf16[768,128]{1,0:T(8,128)(2,1)S(1)}, bf16[768,128]{1,0:T(8,128)(2,1)S(1)}, u32[]{:S(2)}, u32[]{:S(2)}) collective-permute-start(bf16[768,128]{1,0:T(8,128)(2,1)S(1)} %collective-permute-done.1.refs_2_), channel_id=1, source_target_pairs={{0,1},{1,0},{2,3},{3,2},{4,5},{5,4},{6,7},{7,6},{8,9},{9,8},{10,11... | collective-permute-start | bytes 589832 | tf_op jit(solution)/shard_map/ppermute | solution.py:92
  34.6 24.4 %collective-permute-start.17 = (bf16[64,640]{1,0:T(8,128)(2,1)S(1)}, bf16[64,640]{1,0:T(8,128)(2,1)}, u32[]{:S(2)}, u32[]{:S(2)}) collective-permute-start(bf16[64,640]{1,0:T(8,128)(2,1)S(1)} %pad_maximum_fusion.4.refs_0_), channel_id=1, source_target_pairs={{0,16},{16,0},{1,17},{17,1},{2,18},{18,2},{3,19},{19,3},{4,20},{20... | collective-permute-start | bytes 245768 | tf_op jit(solution)/shard_map/ppermute | solution.py:92
  36.1 15.6 %collective-permute-start.16 = (bf16[64,640]{1,0:T(8,128)(2,1)S(1)}, bf16[64,640]{1,0:T(8,128)(2,1)S(1)}, u32[]{:S(2)}, u32[]{:S(2)}) collective-permute-start(bf16[64,640]{1,0:T(8,128)(2,1)S(1)} %pad_maximum_fusion.4.refs_0_), channel_id=1, source_target_pairs={{0,12},{4,8},{8,4},{12,0},{1,13},{5,9},{9,5},{13,1},{2,14},{6,10},... | collective-permute-start | bytes 245768 | tf_op jit(solution)/shard_map/ppermute | solution.py:92
  38.6 13.1 %collective-permute-start.15 = (bf16[64,640]{1,0:T(8,128)(2,1)S(1)}, bf16[64,640]{1,0:T(8,128)(2,1)S(1)}, u32[]{:S(2)}, u32[]{:S(2)}) collective-permute-start(bf16[64,640]{1,0:T(8,128)(2,1)S(1)} %pad_maximum_fusion.4.refs_0_), channel_id=1, source_target_pairs={{0,8},{4,12},{8,0},{12,4},{1,9},{5,13},{9,1},{13,5},{2,10},{6,14},... | collective-permute-start | bytes 245768 | tf_op jit(solution)/shard_map/ppermute | solution.py:92
  40.7 11.0 %collective-permute-start.14 = (bf16[64,640]{1,0:T(8,128)(2,1)S(1)}, bf16[64,640]{1,0:T(8,128)(2,1)S(1)}, u32[]{:S(2)}, u32[]{:S(2)}) collective-permute-start(bf16[64,640]{1,0:T(8,128)(2,1)S(1)} %pad_maximum_fusion.4.refs_0_), channel_id=1, source_target_pairs={{0,4},{4,0},{8,12},{12,8},{1,5},{5,1},{9,13},{13,9},{2,6},{6,2},{1... | collective-permute-start | bytes 245768 | tf_op jit(solution)/shard_map/ppermute | solution.py:92
  47.4 1.6 collective-permute-start.11
  47.4 258.9 %reduce-scatter.2.cloned.1.call-start = ((), (), s32[]{:S(2)}) async-start(), calls=%async_computation.2 | async-start | bytes 1622016 | tf_op jit(solution)/shard_map/reduce_scatter | solution.py:534
  50.6 7.3 %collective-permute-start.12 = (bf16[192,512]{1,0:T(8,128)(2,1)}, bf16[192,512]{1,0:T(8,128)(2,1)}, u32[]{:S(2)}, u32[]{:S(2)}) collective-permute-start(bf16[192,512]{1,0:T(8,128)(2,1)} %add_convert_fusion.18), channel_id=1, source_target_pairs={{0,2},{1,3},{2,0},{3,1},{4,6},{5,7},{6,4},{7,5},{8,10},{9,11},{10,... | collective-permute-start | bytes 589832 | tf_op jit(solution)/shard_map/ppermute | solution.py:92
  51.8 9.7 %collective-permute-start.18 = (bf16[192,640]{1,0:T(8,128)(2,1)S(1)}, bf16[192,640]{1,0:T(8,128)(2,1)S(1)}, u32[]{:S(2)}, u32[]{:S(2)}) collective-permute-start(bf16[192,640]{1,0:T(8,128)(2,1)S(1)} %pad_maximum_fusion.1), channel_id=1, source_target_pairs={{0,16},{16,0},{1,17},{17,1},{2,18},{18,2},{3,19},{19,3},{4,20},{20... | collective-permute-start | bytes 737288 | tf_op jit(solution)/shard_map/ppermute | solution.py:92
  59.0 4.4 %collective-permute-start.13 = (bf16[192,512]{1,0:T(8,128)(2,1)S(1)}, bf16[192,512]{1,0:T(8,128)(2,1)S(1)}, u32[]{:S(2)}, u32[]{:S(2)}) collective-permute-start(bf16[192,512]{1,0:T(8,128)(2,1)S(1)} %add_convert_fusion.17.t1), channel_id=1, source_target_pairs={{0,1},{1,0},{2,3},{3,2},{4,5},{5,4},{6,7},{7,6},{8,9},{9,8},{10,11... | collective-permute-start | bytes 589832 | tf_op jit(solution)/shard_map/ppermute | solution.py:92
  65.4 10.5 %collective-permute-start.21 = (bf16[384,256]{1,0:T(8,128)(2,1)S(1)}, bf16[384,256]{1,0:T(8,128)(2,1)S(1)}, u32[]{:S(2)}, u32[]{:S(2)}) collective-permute-start(bf16[384,256]{1,0:T(8,128)(2,1)S(1)} %get-tuple-element.101.refs_0_), channel_id=1, source_target_pairs={{0,12},{4,8},{8,4},{12,0},{1,13},{5,9},{9,5},{13,1},{2,14},{6,10},... | collective-permute-start | bytes 589832 | tf_op jit(solution)/shard_map/ppermute | solution.py:92
  67.8 23.0 %collective-permute-start.20 = (bf16[384,256]{1,0:T(8,128)(2,1)S(1)}, bf16[384,256]{1,0:T(8,128)(2,1)S(1)}, u32[]{:S(2)}, u32[]{:S(2)}) collective-permute-start(bf16[384,256]{1,0:T(8,128)(2,1)S(1)} %get-tuple-element.101.refs_0_), channel_id=1, source_target_pairs={{0,8},{4,12},{8,0},{12,4},{1,9},{5,13},{9,1},{13,5},{2,10},{6,14},... | collective-permute-start | bytes 589832 | tf_op jit(solution)/shard_map/ppermute | solution.py:92
  67.8 23.0 %collective-permute-start.19 = (bf16[384,256]{1,0:T(8,128)(2,1)S(1)}, bf16[384,256]{1,0:T(8,128)(2,1)S(1)}, u32[]{:S(2)}, u32[]{:S(2)}) collective-permute-start(bf16[384,256]{1,0:T(8,128)(2,1)S(1)} %get-tuple-element.101.refs_0_), channel_id=1, source_target_pairs={{0,4},{4,0},{8,12},{12,8},{1,5},{5,1},{9,13},{13,9},{2,6},{6,2},{1... | collective-permute-start | bytes 589832 | tf_op jit(solution)/shard_map/ppermute | solution.py:92
  98.4 7.0 %collective-permute-start.23 = (bf16[192,512]{1,0:T(8,128)(2,1)S(1)}, bf16[192,512]{1,0:T(8,128)(2,1)S(1)}, u32[]{:S(2)}, u32[]{:S(2)}) collective-permute-start(bf16[192,512]{1,0:T(8,128)(2,1)S(1)} %add_convert_fusion.16), channel_id=1, source_target_pairs={{0,2},{1,3},{2,0},{3,1},{4,6},{5,7},{6,4},{7,5},{8,10},{9,11},{10,... | collective-permute-start | bytes 589832 | tf_op jit(solution)/shard_map/ppermute | solution.py:92
  110.2 3.2 %collective-permute-start.25 = (bf16[16,128]{1,0:T(8,128)(2,1)S(1)}, bf16[16,128]{1,0:T(8,128)(2,1)S(1)}, u32[]{:S(2)}, u32[]{:S(2)}) collective-permute-start(bf16[16,128]{1,0:T(8,128)(2,1)S(1)} %get-tuple-element.109), channel_id=1, source_target_pairs={{0,4},{4,8},{8,12},{1,5},{5,9},{9,13},{2,6},{6,10},{10,14},{3,7},{... | collective-permute-start | bytes 12296 | tf_op jit(solution)/shard_map/ppermute | solution.py:587
  111.9 5.5 %collective-permute-start.26 = (bf16[16,128]{1,0:T(8,128)(2,1)S(1)}, bf16[16,128]{1,0:T(8,128)(2,1)S(1)}, u32[]{:S(2)}, u32[]{:S(2)}) collective-permute-start(bf16[16,128]{1,0:T(8,128)(2,1)S(1)} %get-tuple-element.110), channel_id=1, source_target_pairs={{4,0},{8,4},{12,8},{5,1},{9,5},{13,9},{6,2},{10,6},{14,10},{7,3},{... | collective-permute-start | bytes 12296 | tf_op jit(solution)/shard_map/ppermute | solution.py:587
  118.7 3.7 %collective-permute-start.27 = (f32[8,128]{1,0:T(8,128)S(1)}, f32[8,128]{1,0:T(8,128)S(1)}, u32[]{:S(2)}, u32[]{:S(2)}) collective-permute-start(f32[8,128]{1,0:T(8,128)S(1)} %get-tuple-element.112), channel_id=1, source_target_pairs={{0,16},{16,0},{1,17},{17,1},{2,18},{18,2},{3,19},{19,3},{4,20},{20... | collective-permute-start | bytes 12296 | tf_op jit(solution)/shard_map/ppermute | solution.py:92
  122.4 3.8 %collective-permute-start.28 = (f32[8,128]{1,0:T(8,128)S(1)}, f32[8,128]{1,0:T(8,128)S(1)}, u32[]{:S(2)}, u32[]{:S(2)}) collective-permute-start(f32[8,128]{1,0:T(8,128)S(1)} %maximum_maximum_fusion), channel_id=1, source_target_pairs={{0,4},{4,0},{8,12},{12,8},{1,5},{5,1},{9,13},{13,9},{2,6},{6,2},{1... | collective-permute-start | bytes 12296 | tf_op jit(solution)/shard_map/ppermute | solution.py:92
  126.2 5.1 %collective-permute-start.29 = (f32[8,128]{1,0:T(8,128)S(1)}, f32[8,128]{1,0:T(8,128)S(1)}, u32[]{:S(2)}, u32[]{:S(2)}) collective-permute-start(f32[8,128]{1,0:T(8,128)S(1)} %maximum_maximum_fusion.1), channel_id=1, source_target_pairs={{0,8},{4,12},{8,0},{12,4},{1,9},{5,13},{9,1},{13,5},{2,10},{6,14},... | collective-permute-start | bytes 12296 | tf_op jit(solution)/shard_map/ppermute | solution.py:92
  134.4 7.0 %collective-permute-start.31 = (bf16[192,512]{1,0:T(8,128)(2,1)S(1)}, bf16[192,512]{1,0:T(8,128)(2,1)S(1)}, u32[]{:S(2)}, u32[]{:S(2)}) collective-permute-start(bf16[192,512]{1,0:T(8,128)(2,1)S(1)} %add_convert_fusion.14), channel_id=1, source_target_pairs={{0,2},{1,3},{2,0},{3,1},{4,6},{5,7},{6,4},{7,5},{8,10},{9,11},{10,... | collective-permute-start | bytes 589832 | tf_op jit(solution)/shard_map/ppermute | solution.py:92
  141.5 1.5 collective-permute-start.32
  146.1 7.0 %collective-permute-start.34 = (bf16[192,512]{1,0:T(8,128)(2,1)S(1)}, bf16[192,512]{1,0:T(8,128)(2,1)S(1)}, u32[]{:S(2)}, u32[]{:S(2)}) collective-permute-start(bf16[192,512]{1,0:T(8,128)(2,1)S(1)} %add_convert_fusion.12), channel_id=1, source_target_pairs={{0,2},{1,3},{2,0},{3,1},{4,6},{5,7},{6,4},{7,5},{8,10},{9,11},{10,... | collective-permute-start | bytes 589832 | tf_op jit(solution)/shard_map/ppermute | solution.py:92
  153.2 1.5 collective-permute-start.35
  158.5 7.0 %collective-permute-start.37 = (bf16[192,512]{1,0:T(8,128)(2,1)S(1)}, bf16[192,512]{1,0:T(8,128)(2,1)S(1)}, u32[]{:S(2)}, u32[]{:S(2)}) collective-permute-start(bf16[192,512]{1,0:T(8,128)(2,1)S(1)} %add_convert_fusion.10), channel_id=1, source_target_pairs={{0,2},{1,3},{2,0},{3,1},{4,6},{5,7},{6,4},{7,5},{8,10},{9,11},{10,... | collective-permute-start | bytes 589832 | tf_op jit(solution)/shard_map/ppermute | solution.py:92
  168.5 3.7 %collective-permute-start.39 = (f32[8,128]{1,0:T(8,128)S(1)}, f32[8,128]{1,0:T(8,128)S(1)}, u32[]{:S(2)}, u32[]{:S(2)}) collective-permute-start(f32[8,128]{1,0:T(8,128)S(1)} %slice.140), channel_id=1, source_target_pairs={{0,16},{16,0},{1,17},{17,1},{2,18},{18,2},{3,19},{19,3},{4,20},{20... | collective-permute-start | bytes 12296 | tf_op jit(solution)/shard_map/ppermute | solution.py:92
  172.2 4.0 %collective-permute-start.40 = (f32[72,128]{1,0:T(8,128)S(1)}, f32[72,128]{1,0:T(8,128)S(1)}, u32[]{:S(2)}, u32[]{:S(2)}) collective-permute-start(f32[72,128]{1,0:T(8,128)S(1)} %pad_maximum_fusion.5), channel_id=1, source_target_pairs={{0,4},{4,0},{8,12},{12,8},{1,5},{5,1},{9,13},{13,9},{2,6},{6,2},{1... | collective-permute-start | bytes 110600 | tf_op jit(solution)/shard_map/ppermute | solution.py:92
  176.2 5.8 %collective-permute-start.41 = (f32[72,128]{1,0:T(8,128)S(1)}, f32[72,128]{1,0:T(8,128)S(1)}, u32[]{:S(2)}, u32[]{:S(2)}) collective-permute-start(f32[72,128]{1,0:T(8,128)S(1)} %pad_maximum_fusion.6.own), channel_id=1, source_target_pairs={{0,12},{4,8},{8,4},{12,0},{1,13},{5,9},{9,5},{13,1},{2,14},{6,10},... | collective-permute-start | bytes 110600 | tf_op jit(solution)/shard_map/ppermute | solution.py:92
  183.5 1.5 collective-permute-start.42
  185.0 7.0 %collective-permute-start.43 = (bf16[192,512]{1,0:T(8,128)(2,1)S(1)}, bf16[192,512]{1,0:T(8,128)(2,1)S(1)}, u32[]{:S(2)}, u32[]{:S(2)}) collective-permute-start(bf16[192,512]{1,0:T(8,128)(2,1)S(1)} %add_convert_fusion.8), channel_id=1, source_target_pairs={{0,2},{1,3},{2,0},{3,1},{4,6},{5,7},{6,4},{7,5},{8,10},{9,11},{10,... | collective-permute-start | bytes 589832 | tf_op jit(solution)/shard_map/ppermute | solution.py:92
  192.1 1.5 collective-permute-start.44
  199.7 10.8 %collective-permute-start.45 = (bf16[384,256]{1,0:T(8,128)(2,1)S(1)}, bf16[384,256]{1,0:T(8,128)(2,1)S(1)}, u32[]{:S(2)}, u32[]{:S(2)}) collective-permute-start(bf16[384,256]{1,0:T(8,128)(2,1)S(1)} %get-tuple-element.137), channel_id=1, source_target_pairs={{0,4},{4,0},{8,12},{12,8},{1,5},{5,1},{9,13},{13,9},{2,6},{6,2},{1... | collective-permute-start | bytes 589832 | tf_op jit(solution)/shard_map/ppermute | solution.py:92
  199.7 17.2 %collective-permute-start.46 = (bf16[384,256]{1,0:T(8,128)(2,1)S(1)}, bf16[384,256]{1,0:T(8,128)(2,1)S(1)}, u32[]{:S(2)}, u32[]{:S(2)}) collective-permute-start(bf16[384,256]{1,0:T(8,128)(2,1)S(1)} %get-tuple-element.138), channel_id=1, source_target_pairs={{0,8},{4,12},{8,0},{12,4},{1,9},{5,13},{9,1},{13,5},{2,10},{6,14},... | collective-permute-start | bytes 589832 | tf_op jit(solution)/shard_map/ppermute | solution.py:92
  202.8 14.2 %collective-permute-start.47 = (bf16[384,256]{1,0:T(8,128)(2,1)S(1)}, bf16[384,256]{1,0:T(8,128)(2,1)S(1)}, u32[]{:S(2)}, u32[]{:S(2)}) collective-permute-start(bf16[384,256]{1,0:T(8,128)(2,1)S(1)} %get-tuple-element.139), channel_id=1, source_target_pairs={{0,12},{4,8},{8,4},{12,0},{1,13},{5,9},{9,5},{13,1},{2,14},{6,10},... | collective-permute-start | bytes 589832 | tf_op jit(solution)/shard_map/ppermute | solution.py:92
  220.9 20.6 %collective-permute-start.49 = (bf16[192,512]{1,0:T(8,128)(2,1)}, bf16[192,512]{1,0:T(8,128)(2,1)}, u32[]{:S(2)}, u32[]{:S(2)}) collective-permute-start(bf16[192,512]{1,0:T(8,128)(2,1)} %add_convert_fusion.6), channel_id=1, source_target_pairs={{0,2},{1,3},{2,0},{3,1},{4,6},{5,7},{6,4},{7,5},{8,10},{9,11},{10,... | collective-permute-start | bytes 589832 | tf_op jit(solution)/shard_map/ppermute | solution.py:92
  241.3 10.6 %collective-permute-start.62 = (bf16[256,640]{1,0:T(8,128)(2,1)S(1)}, bf16[256,640]{1,0:T(8,128)(2,1)S(1)}, u32[]{:S(2)}, u32[]{:S(2)}) collective-permute-start(bf16[256,640]{1,0:T(8,128)(2,1)S(1)} %slice.187), channel_id=1, source_target_pairs={{0,16},{16,0},{1,17},{17,1},{2,18},{18,2},{3,19},{19,3},{4,20},{20... | collective-permute-start | bytes 983048 | tf_op jit(solution)/shard_map/ppermute | solution.py:92
  248.2 3.9 %collective-permute-start.66 = (f32[1,512]{1,0:T(1,128)S(1)}, f32[1,512]{1,0:T(1,128)S(1)}, u32[]{:S(2)}, u32[]{:S(2)}) collective-permute-start(f32[1,512]{1,0:T(1,128)S(1)} %get-tuple-element.156), channel_id=1, source_target_pairs={{0,1},{1,0},{2,3},{3,2},{4,5},{5,4},{6,7},{7,6},{8,9},{9,8},{10,11... | collective-permute-start | bytes 6152 | tf_op jit(solution)/shard_map/ppermute | solution.py:92
  252.1 6.7 %collective-permute-start.67 = (f32[1,512]{1,0:T(1,128)S(1)}, f32[1,512]{1,0:T(1,128)S(1)}, u32[]{:S(2)}, u32[]{:S(2)}) collective-permute-start(f32[1,512]{1,0:T(1,128)S(1)} %add.211), channel_id=1, source_target_pairs={{0,2},{1,3},{2,0},{3,1},{4,6},{5,7},{6,4},{7,5},{8,10},{9,11},{10,... | collective-permute-start | bytes 6152 | tf_op jit(solution)/shard_map/ppermute | solution.py:92
  253.7 6.9 %collective-permute-start.63 = (bf16[64,640]{1,0:T(8,128)(2,1)S(1)}, bf16[64,640]{1,0:T(8,128)(2,1)S(1)}, u32[]{:S(2)}, u32[]{:S(2)}) collective-permute-start(bf16[64,640]{1,0:T(8,128)(2,1)S(1)} %get-tuple-element.204), channel_id=1, source_target_pairs={{0,4},{4,0},{8,12},{12,8},{1,5},{5,1},{9,13},{13,9},{2,6},{6,2},{1... | collective-permute-start | bytes 245768 | tf_op jit(solution)/shard_map/ppermute | solution.py:92
  255.9 10.0 %collective-permute-start.65 = (bf16[64,640]{1,0:T(8,128)(2,1)S(1)}, bf16[64,640]{1,0:T(8,128)(2,1)S(1)}, u32[]{:S(2)}, u32[]{:S(2)}) collective-permute-start(bf16[64,640]{1,0:T(8,128)(2,1)S(1)} %get-tuple-element.205), channel_id=1, source_target_pairs={{0,12},{4,8},{8,4},{12,0},{1,13},{5,9},{9,5},{13,1},{2,14},{6,10},... | collective-permute-start | bytes 245768 | tf_op jit(solution)/shard_map/ppermute | solution.py:92
  258.8 9.5 %collective-permute-start.64 = (bf16[64,640]{1,0:T(8,128)(2,1)S(1)}, bf16[64,640]{1,0:T(8,128)(2,1)S(1)}, u32[]{:S(2)}, u32[]{:S(2)}) collective-permute-start(bf16[64,640]{1,0:T(8,128)(2,1)S(1)} %get-tuple-element.206), channel_id=1, source_target_pairs={{0,8},{4,12},{8,0},{12,4},{1,9},{5,13},{9,1},{13,5},{2,10},{6,14},... | collective-permute-start | bytes 245768 | tf_op jit(solution)/shard_map/ppermute | solution.py:92
  260.3 8.1 %collective-permute-start.68 = (f32[38,128]{1,0:T(8,128)S(1)}, f32[38,128]{1,0:T(8,128)S(1)}, u32[]{:S(2)}, u32[]{:S(2)}) collective-permute-start(f32[38,128]{1,0:T(8,128)S(1)} %pad_maximum_fusion.7), channel_id=1, source_target_pairs={{0,16},{16,0},{1,17},{17,1},{2,18},{18,2},{3,19},{19,3},{4,20},{20... | collective-permute-start | bytes 58376 | tf_op jit(solution)/shard_map/ppermute | solution.py:92
  269.1 3.8 %collective-permute-start.69 = (f32[38,128]{1,0:T(8,128)S(1)}, f32[38,128]{1,0:T(8,128)S(1)}, u32[]{:S(2)}, u32[]{:S(2)}) collective-permute-start(f32[38,128]{1,0:T(8,128)S(1)} %fusion.15), channel_id=1, source_target_pairs={{0,4},{4,0},{8,12},{12,8},{1,5},{5,1},{9,13},{13,9},{2,6},{6,2},{1... | collective-permute-start | bytes 58376 | tf_op jit(solution)/shard_map/ppermute | solution.py:92
  269.8 10.5 %collective-permute-start.51 = (bf16[192,512]{1,0:T(8,128)(2,1)}, bf16[192,512]{1,0:T(8,128)(2,1)}, u32[]{:S(2)}, u32[]{:S(2)}) collective-permute-start(bf16[192,512]{1,0:T(8,128)(2,1)} %copy-done.76), channel_id=1, source_target_pairs={{0,1},{1,0},{2,3},{3,2},{4,5},{5,4},{6,7},{7,6},{8,9},{9,8},{10,11... | collective-permute-start | bytes 589832 | tf_op jit(solution)/shard_map/ppermute | solution.py:92
  270.9 11.7 %collective-permute-start.54 = (bf16[256,512]{1,0:T(8,128)(2,1)S(1)}, bf16[256,512]{1,0:T(8,128)(2,1)S(1)}, u32[]{:S(2)}, u32[]{:S(2)}) collective-permute-start(bf16[256,512]{1,0:T(8,128)(2,1)S(1)} %slice.175), channel_id=1, source_target_pairs={{0,16},{16,0},{1,17},{17,1},{2,18},{18,2},{3,19},{19,3},{4,20},{20... | collective-permute-start | bytes 786440 | tf_op jit(solution)/shard_map/ppermute | solution.py:92
  272.9 5.4 %collective-permute-start.70 = (f32[38,128]{1,0:T(8,128)S(1)}, f32[38,128]{1,0:T(8,128)S(1)}, u32[]{:S(2)}, u32[]{:S(2)}) collective-permute-start(f32[38,128]{1,0:T(8,128)S(1)} %add.215), channel_id=1, source_target_pairs={{0,8},{4,12},{8,0},{12,4},{1,9},{5,13},{9,1},{13,5},{2,10},{6,14},... | collective-permute-start | bytes 58376 | tf_op jit(solution)/shard_map/ppermute | solution.py:92
  277.2 9.1 %collective-permute-start.58 = (bf16[256,512]{1,0:T(8,128)(2,1)}, bf16[256,512]{1,0:T(8,128)(2,1)}, u32[]{:S(2)}, u32[]{:S(2)}) collective-permute-start(bf16[256,512]{1,0:T(8,128)(2,1)} %slice.181), channel_id=1, source_target_pairs={{0,16},{16,0},{1,17},{17,1},{2,18},{18,2},{3,19},{19,3},{4,20},{20... | collective-permute-start | bytes 786440 | tf_op jit(solution)/shard_map/ppermute | solution.py:92
  281.2 12.0 %collective-permute-start.52 = (bf16[192,512]{1,0:T(8,128)(2,1)S(1)}, bf16[192,512]{1,0:T(8,128)(2,1)S(1)}, u32[]{:S(2)}, u32[]{:S(2)}) collective-permute-start(bf16[192,512]{1,0:T(8,128)(2,1)S(1)} %add_convert_fusion.4), channel_id=1, source_target_pairs={{0,2},{1,3},{2,0},{3,1},{4,6},{5,7},{6,4},{7,5},{8,10},{9,11},{10,... | collective-permute-start | bytes 589832 | tf_op jit(solution)/shard_map/ppermute | solution.py:92
  282.7 6.8 %collective-permute-start.55 = (bf16[64,512]{1,0:T(8,128)(2,1)S(1)}, bf16[64,512]{1,0:T(8,128)(2,1)S(1)}, u32[]{:S(2)}, u32[]{:S(2)}) collective-permute-start(bf16[64,512]{1,0:T(8,128)(2,1)S(1)} %get-tuple-element.210), channel_id=1, source_target_pairs={{0,4},{4,0},{8,12},{12,8},{1,5},{5,1},{9,13},{13,9},{2,6},{6,2},{1... | collective-permute-start | bytes 196616 | tf_op jit(solution)/shard_map/ppermute | solution.py:92
  283.6 8.2 %collective-permute-start.57 = (bf16[64,512]{1,0:T(8,128)(2,1)S(1)}, bf16[64,512]{1,0:T(8,128)(2,1)S(1)}, u32[]{:S(2)}, u32[]{:S(2)}) collective-permute-start(bf16[64,512]{1,0:T(8,128)(2,1)S(1)} %get-tuple-element.211), channel_id=1, source_target_pairs={{0,12},{4,8},{8,4},{12,0},{1,13},{5,9},{9,5},{13,1},{2,14},{6,10},... | collective-permute-start | bytes 196616 | tf_op jit(solution)/shard_map/ppermute | solution.py:92
  285.4 7.1 %collective-permute-start.56 = (bf16[64,512]{1,0:T(8,128)(2,1)S(1)}, bf16[64,512]{1,0:T(8,128)(2,1)S(1)}, u32[]{:S(2)}, u32[]{:S(2)}) collective-permute-start(bf16[64,512]{1,0:T(8,128)(2,1)S(1)} %get-tuple-element.212), channel_id=1, source_target_pairs={{0,8},{4,12},{8,0},{12,4},{1,9},{5,13},{9,1},{13,5},{2,10},{6,14},... | collective-permute-start | bytes 196616 | tf_op jit(solution)/shard_map/ppermute | solution.py:92
  287.4 6.0 %collective-permute-start.59 = (bf16[64,512]{1,0:T(8,128)(2,1)S(1)}, bf16[64,512]{1,0:T(8,128)(2,1)S(1)}, u32[]{:S(2)}, u32[]{:S(2)}) collective-permute-start(bf16[64,512]{1,0:T(8,128)(2,1)S(1)} %get-tuple-element.207), channel_id=1, source_target_pairs={{0,4},{4,0},{8,12},{12,8},{1,5},{5,1},{9,13},{13,9},{2,6},{6,2},{1... | collective-permute-start | bytes 196616 | tf_op jit(solution)/shard_map/ppermute | solution.py:92
  289.5 8.6 %collective-permute-start.61 = (bf16[64,512]{1,0:T(8,128)(2,1)S(1)}, bf16[64,512]{1,0:T(8,128)(2,1)S(1)}, u32[]{:S(2)}, u32[]{:S(2)}) collective-permute-start(bf16[64,512]{1,0:T(8,128)(2,1)S(1)} %get-tuple-element.208), channel_id=1, source_target_pairs={{0,12},{4,8},{8,4},{12,0},{1,13},{5,9},{9,5},{13,1},{2,14},{6,10},... | collective-permute-start | bytes 196616 | tf_op jit(solution)/shard_map/ppermute | solution.py:92
  291.8 9.6 %collective-permute-start.60 = (bf16[64,512]{1,0:T(8,128)(2,1)S(1)}, bf16[64,512]{1,0:T(8,128)(2,1)S(1)}, u32[]{:S(2)}, u32[]{:S(2)}) collective-permute-start(bf16[64,512]{1,0:T(8,128)(2,1)S(1)} %get-tuple-element.209), channel_id=1, source_target_pairs={{0,8},{4,12},{8,0},{12,4},{1,9},{5,13},{9,1},{13,5},{2,10},{6,14},... | collective-permute-start | bytes 196616 | tf_op jit(solution)/shard_map/ppermute | solution.py:92
  293.2 8.9 %collective-permute-start.53 = (bf16[192,512]{1,0:T(8,128)(2,1)S(1)}, bf16[192,512]{1,0:T(8,128)(2,1)S(1)}, u32[]{:S(2)}, u32[]{:S(2)}) collective-permute-start(bf16[192,512]{1,0:T(8,128)(2,1)S(1)} %add_convert_fusion.3.t1), channel_id=1, source_target_pairs={{0,1},{1,0},{2,3},{3,2},{4,5},{5,4},{6,7},{7,6},{8,9},{9,8},{10,11... | collective-permute-start | bytes 589832 | tf_op jit(solution)/shard_map/ppermute | solution.py:92
  (93 other events, 899.3 us)
Sparse Core Ops, SparseCore 0:
  47.6 48.7 all-gather.1
  232.7 73.5 reduce-scatter.1
where the time goes:
time: 322 us; the launch traced here: 319 us
  waiting for transfers between devices  129 us (40%)
  starting transfers between devices  71.5 us (22%)
  Pallas kernels  47.3 us (15%)
  local copies, waits for them, and re-layouts  40.9 us (13%)
  between operations  15.8 us (5%)
  other arithmetic  14.7 us (5%)
    ppermute x69, waiting for transfers between devices, swap(): return lax.ppermute(value, axis, xor_pairs(lax.axis_size(axis), step))  122 us
    ppermute x69, starting transfers between devices, swap(): return lax.ppermute(value, axis, xor_pairs(lax.axis_size(axis), step))  68 us
    pallas_call x25, Pallas kernels, call(): pl.pallas_call(body, out_shape=outs, in_specs=[pl.BlockSpec(memory_space=...  47.3 us
    unnamed x171, local copies, waits for them, and re-layouts  30.3 us
    convert_element_type x19, other arithmetic, added(): return (left.astype(F32) + right.astype(F32)).astype(BF16)  7.24 us
  transfers between devices with their start and end apart: 73, of which 42 were waited for; matrix products, arithmetic and copies ran while one was open for 7% of the time, Pallas kernels for 10%

commit v1 on v0

--- a/solution.py
+++ b/solution.py
@@ -13,24 +13,28 @@
 EPSILON = 1e-05
 HALO = 16
 BLOCK = 128
-VMEM_BYTES = 12 * 1024 * 1024
-
-
-def call(body, outs, *args, scratch=(), flops=0, vmem=VMEM_BYTES):
-    outs = [jax.ShapeDtypeStruct(shape, dtype) for shape, dtype in outs]
-    moved = sum(a.size * a.dtype.itemsize for a in list(args[1:]) + outs)
+VMEM_BYTES = 16 * 1024 * 1024
+COST = 1
+
+
+def call(body, outs, *args, after=(), scratch=(), results=False, vmem=VMEM_BYTES):
+    first, extra = len(args), len(after)
+
+    def kernel(*refs):
+        body(*refs[:first], *refs[first + extra :])
+
     return pl.pallas_call(
-        body,
-        out_shape=outs,
+        kernel,
+        out_shape=[jax.ShapeDtypeStruct(*out) for out in outs],
         in_specs=[pl.BlockSpec(memory_space=pltpu.SMEM)]
-        + [pl.BlockSpec(memory_space=pltpu.VMEM)] * (len(args) - 1),
-        out_specs=[pl.BlockSpec(memory_space=pltpu.VMEM)] * len(outs),
+        + [pl.BlockSpec(memory_space=pltpu.VMEM)] * (first - 1)
+        + [pl.BlockSpec(memory_space=pl.ANY)] * extra,
+        out_specs=[pl.BlockSpec() if results else pl.BlockSpec(memory_space=pltpu.VMEM)]
+        * len(outs),
         scratch_shapes=list(scratch),
         compiler_params=pltpu.CompilerParams(vmem_limit_bytes=vmem),
-        cost_estimate=pl.CostEstimate(
-            flops=int(flops), bytes_accessed=int(moved), transcendentals=0
-        ),
-    )(*args)
+        cost_estimate=pl.CostEstimate(flops=COST, bytes_accessed=COST, transcendentals=0),
+    )(*args, *after)
 
 
 def dot(left, right):
@@ -96,43 +100,93 @@
     return (left.astype(F32) + right.astype(F32)).astype(BF16)
 
 
+def added_body(idx, left, right, out):
+    out[...] = (left[...].astype(F32) + right[...].astype(F32)).astype(BF16)
+
+
+def added_after(idx, left, right, after):
+    return call(added_body, [(left.shape, left.dtype)], idx, left, right, after=after)[0]
+
+
+def tp_begin(keep, send, idx=None, after=()):
+    other = swap(send, "tp", 1)
+    return added_after(idx, keep, other, after) if after else added(keep, other)
+
+
+def tp_end(idx, total, after=()):
+    other = swap(total, "tp", 2)
+    total = added_after(idx, total, other, after) if after else added(total, other)
+    return total, swap(total, "tp", 1)
+
+
 def tp_sum(keep, send):
-    count = lax.axis_size("tp")
-    total = added(keep, swap(send, "tp", 1))
-    step = 2
-    while step < count:
-        total = added(total, swap(total, "tp", step))
-        step *= 2
-    return total, swap(total, "tp", 1)
-
-
-def place_body(ctx, later, idx, *refs):
-    blocks = refs[: ctx + 2]
-    out = refs[ctx + 2 + later]
-    if later:
-        refs[-1][...] = refs[ctx + 2][...]
-    rows = blocks[0].shape[0]
-    for at in range(2 * ctx):
+    return tp_end(None, tp_begin(keep, send))
+
+
+def place_body(ctx, idx, *refs):
+    out = refs[-1]
+    rows = refs[0].shape[0]
+    blocks = []
+    for ref in refs[:-1]:
+        for at in range(ref.shape[0] // rows):
+            blocks.append(ref[at * rows : (at + 1) * rows, :])
+    for at, block in enumerate(blocks):
         half = idx[2] if at < ctx else 1 - idx[2]
         target = half * ctx + jnp.bitwise_xor(idx[3], at % ctx)
-        if at <= ctx:
-            block = blocks[at][...]
-        else:
-            block = blocks[ctx + 1][(at - ctx - 1) * rows : (at - ctx) * rows, :]
         out[pl.ds(pl.multiple_of(target * rows, rows), rows), :] = block
 
 
+def pack_body(idx, tokens, cot, gains, out):
+    rows = tokens.shape[0]
+    out[:rows, :] = tokens[...]
+    out[rows : 2 * rows, :] = cot[...]
+    rest = gains[...]
+    pieces = []
+    for unused in range(3):
+        piece = rest.astype(BF16).astype(F32)
+        pieces.append(piece)
+        rest = rest - piece
+    pieces.append(jnp.zeros((1, rest.shape[1]), F32))
+    out[2 * rows :, :] = jnp.concatenate(pieces, axis=0).astype(BF16)
+
+
 def features_body(idx, *refs):
-    blocks, gain_blocks = refs[:4], refs[4:8]
-    x_out, cot_out, gains_out = refs[8:]
+    blocks = refs[:4]
+    x_out, cot_out, gains_out = refs[4:]
     rows, features = x_out.shape
     part = features // 4
     for at in range(4):
         target = jnp.bitwise_xor(idx[0], at)
         columns = pl.ds(pl.multiple_of(target * part, part), part)
         x_out[:, columns] = blocks[at][:rows, :]
-        cot_out[:, columns] = blocks[at][rows:, :]
-        gains_out[:, columns] = gain_blocks[at][...]
+        cot_out[:, columns] = blocks[at][rows : 2 * rows, :]
+        pieces = blocks[at][2 * rows :, :].astype(F32)
+        gains_out[:, columns] = (pieces[0:5] + pieces[5:10]) + pieces[10:15]
+
+
+def finish_body(layout, parts, idx, *refs):
+    total = refs[0][...].astype(F32)
+    for ref in refs[1:parts]:
+        total = total + ref[...].astype(F32)
+    column = 0
+    for (kind, width), out in zip(layout, refs[parts:]):
+        if kind == "middle":
+            count = out.shape[0]
+            each = width // count
+            for at in range(count):
+                out[at] = total[:, column + at * each : column + (at + 1) * each]
+        else:
+            out[...] = total[:, column : column + width]
+        column += width
+
+
+def finish_small_body(idx, left, right, gains_out, bias_out, kernel_out):
+    total = left[...] + right[...]
+    gains_out[...] = total[:5]
+    heads, size = bias_out.shape[1:]
+    for head in range(heads):
+        bias_out[:, head, :] = total[5:7, head * size : (head + 1) * size]
+    kernel_out[...] = total[7 : 7 + kernel_out.shape[0]]
 
 
 def wgrad_body(pairs, ordered, ctx, idx, *refs):
@@ -463,20 +517,27 @@
     split(idx, work, keep, send)
 
 
-def feed_back_body(idx, x_ref, d_ref, t1, t2, gains, u, x0, weights, d_out, f_out, du_out, gain_out, last_gain, keep, send, work):
+def feed_back_body(idx, x_ref, d_ref, t1, t2, gains, u, weights, d_out, f_out, du_out, gain_out, keep, send, work):
     join(idx, t1, t2, work)
     grad, gain_grad = norm_pullback(work[...], x_ref[...], gains[1:2, :])
     gain_out[...] = gain_grad
     grad = d_ref[...] + grad
     d_out[...] = grad
     feed_pullback(idx, grad, u, weights, 0, f_out, du_out, keep, send, work)
-    normal, unused = normalized(x0[...].astype(F32))
-    last_gain[...] = jnp.sum(work[...] * normal, axis=0, keepdims=True)
-
-
-def last_body(idx, x_ref, d_ref, t1, t2, gains, out, work):
+
+
+def last_body(idx, x_ref, d_ref, t1, t2, gains, two, three, four, five, bias, kernel, out, small, work, each):
     join(idx, t1, t2, work)
-    grad, unused = norm_pullback(work[...], x_ref[...].astype(F32), gains[0:1, :])
+    grad, gain_grad = norm_pullback(work[...], x_ref[...].astype(F32), gains[0:1, :])
+    for at, row in enumerate((gain_grad, two[...], three[...], four[...], five[...])):
+        each[at : at + 1, :] = row
+    part = out.shape[1]
+    own = pl.ds(pl.multiple_of(idx[0] * part, part), part)
+    taps = kernel.shape[0]
+    small[:5, :] = each[:5, own]
+    small[5:7, :] = bias[...]
+    small[7 : 7 + taps, :] = kernel[...]
+    small[7 + taps :, :] = jnp.zeros((small.shape[0] - 7 - taps, part), F32)
     work[...] = d_ref[...] + grad
     width = out.shape[1]
     out[...] = work[:, pl.ds(pl.multiple_of(idx[0] * width, width), width)]
@@ -489,21 +550,22 @@
     return lax.axis_size("fsdp") == 2
 
 
-def gathered(idx, shard, later=None):
+def gathered(idx, shard, after=()):
     if not paired_mesh():
-        whole = lax.all_gather(shard, FRAMES, axis=0, tiled=True)
-        return whole if later is None else (whole, later)
+        return lax.all_gather(shard, FRAMES, axis=0, tiled=True), shard
     ctx = lax.axis_size("ctx")
+    if after:
+        shard = held(idx, shard, after)
     mine = [shard] + [swap(shard, "ctx", step) for step in range(1, ctx)]
-    theirs = [swap(shard, "fsdp", 1), swap(jnp.concatenate(mine[1:], axis=0), "fsdp", 1)]
+    if after:
+        mark = jnp.concatenate(mine, axis=0)
+        theirs = [swap(mark, "fsdp", 1)]
+    else:
+        mark = jnp.concatenate(mine[1:], axis=0)
+        theirs = [swap(shard, "fsdp", 1), swap(mark, "fsdp", 1)]
     rows, width = shard.shape
     outs = [((2 * ctx * rows, width), BF16)]
-    handed = [] if later is None else [later]
-    outs += [(later.shape, later.dtype)] if handed else []
-    results = call(
-        functools.partial(place_body, ctx, len(handed)), outs, idx, *mine, *theirs, *handed
-    )
-    return results if handed else results[0]
+    return call(functools.partial(place_body, ctx), outs, idx, *mine, *theirs)[0], mark
 
 
 def features_whole(value):
@@ -516,30 +578,67 @@
     width = sum(right.shape[1] for unused, right in pairs)
     flat = [array for pair in pairs for array in pair]
     ctx = lax.axis_size("ctx")
-    flops = sum(2 * left.shape[0] * depth * right.shape[1] for left, right in pairs)
     return call(
         functools.partial(wgrad_body, len(pairs), ordered, ctx),
         [((depth, width), BF16)],
         idx,
         *flat,
         scratch=[pltpu.VMEM((8, 128) if ordered else (depth, width), BF16)],
-        flops=flops,
     )[0]
 
 
-def scattered(idx, pairs, direct):
-    direct = direct and paired_mesh()
-    grads = weight_grads(idx, pairs, not direct)
-    if not direct:
-        return lax.psum_scatter(grads, FRAMES, scatter_dimension=0, tiled=True).astype(F32)
+def scattered(idx, pairs, layout):
+    grads = weight_grads(idx, pairs, not paired_mesh())
+    rows = grads.shape[0] // lax.axis_size(FRAMES)
+
+    def formed(values):
+        turns = {"rows": lambda v: v, "turned": lambda v: v.T, "middle": lambda v: v.swapaxes(0, 1)}
+        return [turns[kind](value) for (kind, unused, unused), value in zip(layout, values)]
+
+    if not paired_mesh():
+        total = lax.psum_scatter(grads, FRAMES, scatter_dimension=0, tiled=True).astype(F32)
+
+        def whole(after=()):
+            values, column = [], 0
+            for kind, count, width in layout:
+                value = total[:, column : column + width]
+                if kind == "middle":
+                    value = value.reshape(rows, count, width // count).swapaxes(0, 1)
+                values.append(value)
+                column += width
+            return formed(values)
+
+        return grads, grads, lambda after=(): (grads, whole)
     ctx = lax.axis_size("ctx")
     half = grads.shape[0] // 2
-    rows = half // ctx
-    total = added(grads[:half], swap(grads[half:], "fsdp", 1))
-    parts = [total[:rows]]
-    for step in range(1, ctx):
-        parts.append(swap(total[step * rows : (step + 1) * rows], "ctx", step))
-    return sum(part.astype(F32) for part in parts)
+    other = swap(grads[half:], "fsdp", 1)
+
+    def along(after=()):
+        total = added_after(idx, grads[:half], other, after)
+        parts = [total[:rows]]
+        for step in range(1, ctx):
+            parts.append(swap(total[step * rows : (step + 1) * rows], "ctx", step))
+
+        def finish(after=()):
+            shapes = [
+                ((count, rows, width // count) if kind == "middle" else (rows, width), F32)
+                for kind, count, width in layout
+            ]
+            kinds = [(kind, width) for kind, unused, width in layout]
+            body = functools.partial(finish_body, kinds, ctx)
+            return formed(call(body, shapes, idx, *parts, after=after, results=True))
+
+        return total, finish
+
+    return grads, other, along
+
+
+def hold_body(idx, value, out):
+    out[...] = value[...]
+
+
+def held(idx, value, after):
+    return call(hold_body, [(value.shape, value.dtype)], idx, value, after=after)[0]
 
 
 def over_frames(value, merge):
@@ -549,10 +648,6 @@
             value = merge(value, swap(value, axis, step))
             step *= 2
     return value
-
-
-def summed(value):
-    return over_frames(value, lambda left, right: left + right)
 
 
 def pooled(stats, rows):
@@ -638,35 +733,31 @@
         [tp_at, tp_at % 2, lax.axis_index("fsdp"), ctx_at]
     ).astype(jnp.int32)
 
-    last_shard = jnp.concatenate(
-        [
-            gating_map.reshape(shard, 2 * channels),
-            mixing_map.T,
-            second_expand,
-            second_shrink.T,
-        ],
-        axis=1,
-    )
-    one, last_shard = gathered(
-        idx, jnp.concatenate([first_expand, first_shrink.T], axis=1), last_shard
-    )
+    one, one_mark = gathered(idx, jnp.concatenate([first_expand, first_shrink.T], axis=1))
+    frames = call(
+        pack_body, [((2 * rows + 16, part), BF16)], idx, tokens, cotangent, layer_gains
+    )[0]
     x0, cot, gains = call(
         features_body,
         [((rows, features), BF16), ((rows, features), BF16), ((5, features), F32)],
         idx,
-        *features_whole(jnp.concatenate([tokens, cotangent], axis=0)),
-        *features_whole(layer_gains),
+        *features_whole(frames),
     )
     bias = position_bias.reshape(2, local)
     params = jnp.stack([batch_scale, batch_shift])
     tables = angle_tables(ctx_at * rows, rows, width, features)
-    two = gathered(
-        idx,
-        jnp.concatenate(
-            [attend_input.reshape(shard, 3 * local), position_map, attend_output.T], axis=1
-        ),
-    )
-    three = lax.all_gather(last_shard, FRAMES, axis=0, tiled=True)
+    thirds = [attend_input[:, at] for at in range(3)]
+    two, two_mark = gathered(
+        idx,
+        jnp.concatenate(thirds + [position_map, attend_output.T], axis=1),
+        [one_mark],
+    )
+    halves_in = [gating_map[:, at] for at in range(2)]
+    three, three_mark = gathered(
+        idx,
+        jnp.concatenate(halves_in + [mixing_map.T, second_expand, second_shrink.T], axis=1),
+        [two_mark],
+    )
     at_pos, at_out = 3 * local, 4 * local
     at_mix, at_two = 2 * channels, 3 * channels
 
@@ -675,27 +766,25 @@
     piece = ((rows // 2, features), BF16)
     gain_row = ((1, features), F32)
     work = pltpu.VMEM((rows, features), F32)
-    feed_flops = 4 * rows * features * hidden
-
-    feed_outs = [packed, ((rows, hidden), F32), ((rows, hidden), BF16), piece, piece]
+    inner_shape = (rows, hidden)
+
     z1, u1, h1, keep, send = call(
         functools.partial(feed_body, 0, 0, False),
-        feed_outs,
+        [packed, (inner_shape, F32), (inner_shape, BF16), piece, piece],
         idx,
         x0,
         gains,
         one,
+        after=[two_mark],
         scratch=[work],
-        flops=feed_flops,
-    )
-    t1, t2 = tp_sum(keep, send)
+    )
+    t1, t2 = tp_end(idx, tp_begin(keep, send), [three_mark, two])
     embed, relative = call(
         functools.partial(relative_body, at_pos),
         [((width, features), BF16), ((width, local), BF16)],
         idx,
         *tables,
         two,
-        flops=2 * width * features * local,
     )
     per_head = ((rows, local), BF16)
     x1, z2, qa, qb, kv = call(
@@ -709,7 +798,6 @@
         two,
         bias,
         scratch=[work],
-        flops=6 * rows * features * local,
     )
     pairs = [kv] + [swap(kv, "ctx", step) for step in range(1, ctx)]
     position = call(
@@ -718,7 +806,7 @@
         idx,
         qb,
         relative,
-        flops=2 * rows * (length + BLOCK) * local * 8,
+        after=[three],
     )[0]
     whole_pairs = pltpu.VMEM((length, 2 * local), BF16)
     p, mixed, keep, send = call(
@@ -730,13 +818,19 @@
         position,
         two,
         scratch=[whole_pairs, work],
-        flops=4 * rows * length * local * 8,
     )
     t1, t2 = tp_sum(keep, send)
     edge = ((HALO, channels), BF16)
     x2, z3, paired, glu, first, last = call(
         conv_in_body,
-        [stream, packed, ((rows, 2 * channels), F32), ((rows, channels), BF16), edge, edge],
+        [
+            stream,
+            packed,
+            ((rows, 2 * channels), F32),
+            ((rows, channels), BF16),
+            edge,
+            edge,
+        ],
         idx,
         x1,
         t1,
@@ -744,7 +838,6 @@
         gains,
         three,
         scratch=[work],
-        flops=4 * rows * features * channels,
     )
     low, high = neighbours(first, last)
     padded = pltpu.VMEM((rows + 2 * HALO, channels), F32)
@@ -768,12 +861,11 @@
         params,
         three,
         scratch=[work],
-        flops=2 * rows * features * channels,
     )
     t1, t2 = tp_sum(keep, send)
     x3, z4, u2, h2, keep, send = call(
         functools.partial(feed_body, 3, at_two, True),
-        [stream] + feed_outs,
+        [stream, packed, (inner_shape, F32), (inner_shape, BF16), piece, piece],
         idx,
         x2,
         t1,
@@ -781,12 +873,19 @@
         gains,
         three,
         scratch=[work],
-        flops=feed_flops,
     )
     t1, t2 = tp_sum(keep, send)
     outputs, d4, gain_five, f4, du2, keep, send = call(
         functools.partial(final_body, at_two),
-        [((rows, part), BF16), stream, gain_row, packed, ((rows, hidden), BF16), piece, piece],
+        [
+            ((rows, part), BF16),
+            stream,
+            gain_row,
+            packed,
+            (inner_shape, BF16),
+            piece,
+            piece,
+        ],
         idx,
         x3,
         t1,
@@ -796,12 +895,21 @@
         u2,
         three,
         scratch=[work],
-        flops=feed_flops,
-    )
-    t1, t2 = tp_sum(keep, send)
+    )
+    total = tp_begin(keep, send)
+    made_rear, other_rear, rear = scattered(
+        idx, [(z4, du2), (f4, h2)], [("rows", 1, hidden), ("turned", 1, hidden)]
+    )
+    t1, t2 = tp_end(idx, total, [made_rear])
     d3, f3, da, edges, gain_four = call(
         functools.partial(conv_back_body, at_mix),
-        [stream, packed, ((rows, channels), F32), ((8 + 4 * HALO, channels), F32), gain_row],
+        [
+            stream,
+            packed,
+            ((rows, channels), F32),
+            ((8 + 4 * HALO, channels), F32),
+            gain_row,
+        ],
         idx,
         x3,
         d4,
@@ -812,13 +920,18 @@
         params,
         three,
         scratch=[work],
-        flops=2 * rows * features * channels,
     )
     own, near, far = edges_summed(edges)
     counted = rows * lax.axis_size(FRAMES)
     sums, dc, dg, keep, send = call(
         functools.partial(gate_back_body, ctx, counted),
-        [((8, channels), F32), ((rows, channels), BF16), ((rows, 2 * channels), BF16), piece, piece],
+        [
+            ((8, channels), F32),
+            ((rows, channels), BF16),
+            ((rows, 2 * channels), BF16),
+            piece,
+            piece,
+        ],
         idx,
         da,
         q,
@@ -830,10 +943,10 @@
         depth_kernel,
         paired,
         three,
+        after=[other_rear],
         scratch=[padded, work],
-        flops=4 * rows * features * channels,
-    )
-    t1, t2 = tp_sum(keep, send)
+    )
+    total = tp_begin(keep, send)
     kernel_grad = call(
         taps_body,
         [(depth_kernel.shape, F32)],
@@ -844,7 +957,13 @@
         dc,
         scratch=[padded],
     )[0]
-    middle = scattered(idx, [(z3, dg), (f3, act), (z4, du2), (f4, h2)], False)
+    made_middle, other_middle, middle = scattered(
+        idx,
+        [(z3, dg), (f3, act)],
+        [("middle", 2, 2 * channels), ("turned", 1, channels)],
+    )
+    rear_total, rear = rear([total])
+    t1, t2 = tp_end(idx, total, [made_middle, kernel_grad, rear_total])
     pair_block = ((rows, 2 * local), BF16)
     results = call(
         functools.partial(attend_back_body, heads, ctx, at_out),
@@ -861,7 +980,6 @@
         qa,
         *pairs,
         scratch=[whole_pairs, whole_pairs, pltpu.VMEM((rows, local), BF16), work],
-        flops=8 * rows * length * local * 4,
     )
     d2, f2, gain_three, ds, dqa = results[:5]
     pair_grads = [results[5]] + [
@@ -875,8 +993,8 @@
         qb,
         relative,
         scratch=[pltpu.VMEM((BLOCK, length + BLOCK), F32), pltpu.VMEM((width, local), F32)],
-        flops=4 * rows * (length + BLOCK) * local * 8,
-    )
+    )
+    rear_expand, rear_shrink = rear([ds])
     dp, bias_grad, keep, send = call(
         functools.partial(attend_out_body, ctx),
         [((rows, 3 * local), BF16), ((2, local), F32), piece, piece],
@@ -885,14 +1003,21 @@
         dqb,
         *pair_grads,
         two,
+        after=[rear_expand, other_middle],
         scratch=[work],
-        flops=6 * rows * features * local,
-    )
-    t1, t2 = tp_sum(keep, send)
-    inner = scattered(idx, [(z2, dp), (embed, dr), (f2, mixed)], True)
-    d1, f1, du1, gain_two, gain_one, keep, send = call(
+    )
+    total = tp_begin(keep, send)
+    made_inner, other_inner, inner = scattered(
+        idx,
+        [(z2, dp), (embed, dr), (f2, mixed)],
+        [("middle", 3, 3 * local), ("rows", 1, local), ("turned", 1, local)],
+    )
+    middle_total, middle = middle([total])
+    t1, t2 = tp_end(idx, total, [made_inner, middle_total])
+    gate_grad, mix_grad = middle([total])
+    d1, f1, du1, gain_two, keep, send = call(
         feed_back_body,
-        [stream, packed, ((rows, hidden), BF16), gain_row, gain_row, piece, piece],
+        [stream, ((rows, features), BF16), (inner_shape, BF16), gain_row, piece, piece],
         idx,
         x1,
         d2,
@@ -900,54 +1025,70 @@
         t2,
         gains,
         u1,
-        x0,
         one,
+        after=[mix_grad],
         scratch=[work],
-        flops=feed_flops,
-    )
-    t1, t2 = tp_sum(keep, send)
-    front_b = scattered(idx, [(f1, h1)], True)
-    front_a = scattered(idx, [(z1, du1)], True)
-    step = 1
-    while step < tp:
-        gain_one = gain_one + swap(gain_one, "tp", step)
-        step *= 2
-    rows_grad = lax.dynamic_slice_in_dim(
-        jnp.concatenate([gain_one, gain_two, gain_three, gain_four, gain_five], axis=0),
-        tp_at * part,
-        part,
-        axis=1,
-    )
-    small = summed(jnp.concatenate([rows_grad, bias_grad, kernel_grad], axis=0))
+    )
+    made_front, unused, front = scattered(
+        idx, [(z1, du1), (f1, h1)], [("rows", 1, hidden), ("turned", 1, hidden)]
+    )
+    total = tp_begin(keep, send, idx, [made_front, other_inner])
+    inner_total, inner = inner([total])
+    t1, t2 = tp_end(idx, total, [inner_total])
     taps = depth_kernel.shape[0]
-    tokens_grad = call(
+    tokens_grad, small = call(
         last_body,
-        [((rows, part), F32)],
+        [((rows, part), F32), ((-(-(7 + taps) // 8) * 8, part), F32)],
         idx,
         x0,
         d1,
         t1,
         t2,
         gains,
-        scratch=[work],
-    )[0]
+        gain_two,
+        gain_three,
+        gain_four,
+        gain_five,
+        bias_grad,
+        kernel_grad,
+        scratch=[work, pltpu.VMEM((8, features), F32)],
+    )
+    steps = [
+        (axis, step)
+        for axis in ("fsdp", "ctx")
+        for step in (1, 2, 4, 8)
+        if step < lax.axis_size(axis)
+    ]
+    front_total, front = front([small])
+    for axis, step in steps[:-1]:
+        small = small + swap(small, axis, step)
+    qkv_grad, map_grad, out_grad = inner([front_total])
+    gains_grad, bias_grad, kernel_grad = call(
+        finish_small_body,
+        [((5, part), F32), ((2, heads, size), F32), ((taps, channels), F32)],
+        idx,
+        small,
+        swap(small, *steps[-1]),
+        results=True,
+    )
+    front_expand, front_shrink = front()
     return (
         outputs,
         tokens_grad,
-        front_a,
-        front_b.T,
-        inner[:, :at_pos].reshape(shard, 3, local),
-        inner[:, at_pos:at_out],
-        small[5:7].reshape(2, heads, size),
-        inner[:, at_out:].T,
-        middle[:, :at_mix].reshape(shard, 2, channels),
-        small[7 : 7 + taps],
+        front_expand,
+        front_shrink,
+        qkv_grad,
+        map_grad,
+        bias_grad,
+        out_grad,
+        gate_grad,
+        kernel_grad,
         sums[0],
         sums[1],
-        middle[:, at_mix:at_two].T,
-        middle[:, at_two : at_two + hidden],
-        middle[:, at_two + hidden :].T,
-        small[:5],
+        mix_grad,
+        rear_expand,
+        rear_shrink,
+        gains_grad,
     )
 
 

time: 322 us -> 285 us (0.89)
  Pallas kernels: 47.3 us -> 69.8 us
  local copies, waits for them, and re-layouts: 40.9 us -> 18.7 us
  waiting for transfers between devices: 129 us -> 110 us
  between operations: 15.8 us -> 1.77 us
  other arithmetic: 14.7 us -> 2.59 us
  starting transfers between devices: 71.5 us -> 77.3 us
    pallas_call x25 -> x44, Pallas kernels: 47.3 us -> 69.8 us  [call(): pl.pallas_call(kernel, out_shape=[jax.ShapeDtypeStruct(*out) for out in o...]
    ppermute x69 -> x71, waiting for transfers between devices: 122 us -> 106 us  [swap(): return lax.ppermute(value, axis, xor_pairs(lax.axis_size(axis), step))]
    unnamed x171 -> x73, local copies, waits for them, and re-layouts: 30.3 us -> 14.5 us
    convert_element_type x19 -> x10, other arithmetic: 7.24 us -> 0.54 us  [added(): return (left.astype(F32) + right.astype(F32)).astype(BF16)]
    ppermute x69 -> x71, starting transfers between devices: 68 us -> 74.7 us  [swap(): return lax.ppermute(value, axis, xor_pairs(lax.axis_size(axis), step))]
  transfers between devices with their start and end apart: 73 -> 73, of which waited for: 42 -> 39; matrix products, arithmetic and copies ran while one was open for 7% -> 3% of each run, Pallas kernels for 10% -> 19%
where the time goes in v1:
time: 285 us; the launch traced here: 280 us
  waiting for transfers between devices  110 us (39%)
  starting transfers between devices  77.3 us (27%)
  Pallas kernels  69.8 us (24%)
  local copies, waits for them, and re-layouts  18.7 us (7%)
    ppermute x71, waiting for transfers between devices, swap(): return lax.ppermute(value, axis, xor_pairs(lax.axis_size(axis), step))  106 us
    ppermute x71, starting transfers between devices, swap(): return lax.ppermute(value, axis, xor_pairs(lax.axis_size(axis), step))  74.7 us
    pallas_call x44, Pallas kernels, call(): pl.pallas_call(kernel, out_shape=[jax.ShapeDtypeStruct(*out) for out in o...  69.8 us
    unnamed x73, local copies, waits for them, and re-layouts  14.5 us
  transfers between devices with their start and end apart: 73, of which 39 were waited for; matrix products, arithmetic and copies ran while one was open for 3% of the time, Pallas kernels for 19%

profile of v1, /device:TPU:0, one launch (start us, length us, event | category | flops | bytes accessed | tf_op | source)
XLA Modules:
  0.0 280.0 jit_solution(2431287480323781376)
XLA Ops:
  1.6 5.1 %collective-permute-start.5 = (bf16[64,1024]{1,0:T(8,128)(2,1)S(1)}, bf16[64,1024]{1,0:T(8,128)(2,1)S(1)}, u32[]{:S(2)}, u32[]{:S(2)}) collective-permute-start(bf16[64,1024]{1,0:T(8,128)(2,1)S(1)} %pad_maximum_fusion.2.refs_1_), channel_id=1, source_target_pairs={{0,12},{4,8},{8,4},{12,0},{1,13},{5,9},{9,5},{13,1},{2,14},{6,10},... | collective-permute-start | bytes 393224 | tf_op jit(solution)/shard_map/ppermute | solution.py:96
  10.5 1.7 collective-permute-start.1
  18.4 2.7 collective-permute-start.10
  21.2 1.7 collective-permute-start.8
  23.0 1.5 collective-permute-start.7
  25.4 3.0 %collective-permute-done.9.refs_3_ = bf16[64,640]{1,0:T(8,128)(2,1)S(1)} collective-permute-done((bf16[64,640]{1,0:T(8,128)(2,1)S(1)}, bf16[64,640]{1,0:T(8,128)(2,1)S(1)}, u32[]{:S(2)}, u32[]{:S(2)}) %collective-permute-start.9) | collective-permute-done | bytes 81952 | tf_op jit(solution)/shard_map/ppermute | solution.py:96
  28.4 1.6 collective-permute-start.6
  30.5 2.4 collective-permute-start.15
  33.3 1.7 collective-permute-start.13
  42.6 1.5 shard_map.283
  44.9 3.9 %collective-permute-done.14.refs_3_ = bf16[64,1408]{1,0:T(8,128)(2,1)S(1)} collective-permute-done((bf16[64,1408]{1,0:T(8,128)(2,1)S(1)}, bf16[64,1408]{1,0:T(8,128)(2,1)S(1)}, u32[]{:S(2)}, u32[]{:S(2)}) %collective-permute-start.14) | collective-permute-done | bytes 180256 | tf_op jit(solution)/shard_map/ppermute | solution.py:96
  50.5 5.0 %collective-permute-done.12.refs_2_ = bf16[192,512]{1,0:T(8,128)(2,1)S(1)} collective-permute-done((bf16[192,512]{1,0:T(8,128)(2,1)S(1)}, bf16[192,512]{1,0:T(8,128)(2,1)S(1)}, u32[]{:S(2)}, u32[]{:S(2)}) %collective-permute-start.12) | collective-permute-done | bytes 196640 | tf_op jit(solution)/shard_map/ppermute | solution.py:96
  58.8 1.5 collective-permute-start.20
  60.3 2.9 %collective-permute-start.18 = (bf16[384,256]{1,0:T(8,128)(2,1)S(1)}, bf16[384,256]{1,0:T(8,128)(2,1)S(1)}, u32[]{:S(2)}, u32[]{:S(2)}) collective-permute-start(bf16[384,256]{1,0:T(8,128)(2,1)S(1)} %get-tuple-element.111.refs_2_.refs_9_), channel_id=1, source_target_pairs={{0,4},{4,0},{8,12},{12,8},{1,5},{5,1},{9,13},{13,9},{2,6},{6,2},{1... | collective-permute-start | bytes 589832 | tf_op jit(solution)/shard_map/ppermute | solution.py:96
  66.3 3.1 %shard_map.290.refs_6_ = f32[2,384,1536]{2,1,0:T(8,128)S(1)} custom-call(s32[4]{0:T(128)S(1)} %pad_add_fusion.refs_0_, bf16[384,128]{1,0:T(8,128)(2,1)S(1)} %get-tuple-element.112.refs_1_.refs_2_, bf16[1920,128]{1,0:T(8,128)(2,1)S(1)} %get-tuple-element.113.refs_2_.refs_3_, bf16[512,1408]{1,0:T(8,128)(2,1)S(1)} %shard_map.289.refs_3_.refs_5_.refs_4_.refs_7_.refs_8_.refs_10_), custom_call_target="tpu_custom_call" | custom-call | flops 1 | bytes 1 | tf_op jit(solution)/shard_map/pallas_call | solution.py:26
  69.5 7.8 %collective-permute-done.19.refs_4_.refs_11_ = bf16[384,256]{1,0:T(8,128)(2,1)S(1)} collective-permute-done((bf16[384,256]{1,0:T(8,128)(2,1)S(1)}, bf16[384,256]{1,0:T(8,128)(2,1)S(1)}, u32[]{:S(2)}, u32[]{:S(2)}) %collective-permute-start.19) | collective-permute-done | bytes 196640 | tf_op jit(solution)/shard_map/ppermute | solution.py:96
  77.3 4.6 %shard_map.291 = (bf16[2,384,1536]{2,1,0:T(8,128)(2,1)S(1)}, bf16[384,128]{1,0:T(8,128)(2,1)S(1)}, bf16[192,512]{1,0:T(8,128)(2,1)S(1)}, bf16[192,512]{1,0:T(8,128)(2,1)S(1)}) custom-call(s32[4]{0:T(128)S(1)} %pad_add_fusion.refs_0_, bf16[384,128]{1,0:T(8,128)(2,1)S(1)} %get-tuple-element.110.refs_1_.refs_8_, ...), custom_call_target="tpu_custom_call" | custom-call | flops 1 | bytes 1 | tf_op jit(solution)/shard_map/pallas_call | solution.py:26
  82.0 1.4 collective-permute-done.22
  84.0 6.5 %collective-permute-done.23 = bf16[192,512]{1,0:T(8,128)(2,1)S(1)} collective-permute-done((bf16[192,512]{1,0:T(8,128)(2,1)S(1)}, bf16[192,512]{1,0:T(8,128)(2,1)S(1)}, u32[]{:S(2)}, u32[]{:S(2)}) %collective-permute-start.23) | collective-permute-done | bytes 196640 | tf_op jit(solution)/shard_map/ppermute | solution.py:96
  90.6 1.4 collective-permute-done.24.refs_3_
  96.1 4.2 %collective-permute-done.26.refs_3_ = bf16[16,128]{1,0:T(8,128)(2,1)S(1)} collective-permute-done((bf16[16,128]{1,0:T(8,128)(2,1)S(1)}, bf16[16,128]{1,0:T(8,128)(2,1)S(1)}, u32[]{:S(2)}, u32[]{:S(2)}) %collective-permute-start.26) | collective-permute-done | bytes 4128 | tf_op jit(solution)/shard_map/ppermute | solution.py:682
  102.5 2.8 collective-permute-done.27
  105.2 2.0 collective-permute-start.28
  107.2 1.7 collective-permute-done.28
  108.9 3.4 %collective-permute-start.29 = (f32[8,128]{1,0:T(8,128)S(1)}, f32[8,128]{1,0:T(8,128)S(1)}, u32[]{:S(2)}, u32[]{:S(2)}) collective-permute-start(f32[8,128]{1,0:T(8,128)S(1)} %maximum_maximum_fusion.1), channel_id=1, source_target_pairs={{0,8},{4,12},{8,0},{12,4},{1,9},{5,13},{9,1},{13,5},{2,10},{6,14},... | collective-permute-start | bytes 12296 | tf_op jit(solution)/shard_map/ppermute | solution.py:96
  112.4 1.6 collective-permute-done.29
  114.9 1.4 collective-permute-done.30
  117.0 6.4 %collective-permute-done.31 = bf16[192,512]{1,0:T(8,128)(2,1)S(1)} collective-permute-done((bf16[192,512]{1,0:T(8,128)(2,1)S(1)}, bf16[192,512]{1,0:T(8,128)(2,1)S(1)}, u32[]{:S(2)}, u32[]{:S(2)}) %collective-permute-start.31) | collective-permute-done | bytes 196640 | tf_op jit(solution)/shard_map/ppermute | solution.py:96
  123.6 1.4 collective-permute-done.32.refs_3_
  125.0 1.5 shard_map.295
  128.7 6.4 %collective-permute-done.34 = bf16[192,512]{1,0:T(8,128)(2,1)S(1)} collective-permute-done((bf16[192,512]{1,0:T(8,128)(2,1)S(1)}, bf16[192,512]{1,0:T(8,128)(2,1)S(1)}, u32[]{:S(2)}, u32[]{:S(2)}) %collective-permute-start.34) | collective-permute-done | bytes 196640 | tf_op jit(solution)/shard_map/ppermute | solution.py:96
  135.3 1.4 collective-permute-done.35.refs_3_
  136.7 2.3 shard_map.296
  142.4 5.1 %collective-permute-done.37.refs_2_ = bf16[192,512]{1,0:T(8,128)(2,1)S(1)} collective-permute-done((bf16[192,512]{1,0:T(8,128)(2,1)S(1)}, bf16[192,512]{1,0:T(8,128)(2,1)S(1)}, u32[]{:S(2)}, u32[]{:S(2)}) %collective-permute-start.37) | collective-permute-done | bytes 196640 | tf_op jit(solution)/shard_map/ppermute | solution.py:96
  148.1 1.4 collective-permute-done.38.refs_4_
  153.1 1.5 collective-permute-done.39
  154.6 1.5 collective-permute-start.40
  156.1 2.5 collective-permute-done.40.refs_4_
  158.6 2.4 collective-permute-start.41
  161.0 4.6 %collective-permute-done.42.refs_11_.refs_2_ = bf16[256,1024]{1,0:T(8,128)(2,1)S(1)} collective-permute-done((bf16[256,1024]{1,0:T(8,128)(2,1)S(1)}, bf16[256,1024]{1,0:T(8,128)(2,1)S(1)}, u32[]{:S(2)}, u32[]{:S(2)}) %collective-permute-start.42) | collective-permute-done | bytes 524320 | tf_op jit(solution)/shard_map/ppermute | solution.py:96
  165.7 1.4 shard_map.300
  170.6 2.4 collective-permute-start.51
  173.6 3.0 %collective-permute-done.44.refs_2_ = bf16[192,512]{1,0:T(8,128)(2,1)S(1)} collective-permute-done((bf16[192,512]{1,0:T(8,128)(2,1)S(1)}, bf16[192,512]{1,0:T(8,128)(2,1)S(1)}, u32[]{:S(2)}, u32[]{:S(2)}) %collective-permute-start.44) | collective-permute-done | bytes 196640 | tf_op jit(solution)/shard_map/ppermute | solution.py:96
  178.8 15.1 %shard_map.305 = (f32[384,512]{1,0:T(8,128)S(1)}, bf16[384,512]{1,0:T(8,128)(2,1)S(1)}, f32[1,512]{1,0:T(1,128)S(1)}, bf16[2,384,1536]{2,1,0:T(8,128)(2,1)S(1)},...) custom-call(s32[4]{0:T(128)S(1)} %pad_add_fusion.refs_0_, ...), custom_call_target="tpu_custom_call" | custom-call | flops 1 | bytes 1 | tf_op jit(solution)/shard_map/pallas_call | solution.py:26
  193.8 1.5 collective-permute-start.46
  195.4 1.5 collective-permute-start.47
  196.9 1.4 collective-permute-start.48
  198.9 5.2 %shard_map.306 = (f32[384,128]{1,0:T(8,128)S(1)}, bf16[1920,128]{1,0:T(8,128)(2,1)S(1)}) custom-call(s32[4]{0:T(128)S(1)} %pad_add_fusion.refs_0_, bf16[2,384,1536]{2,1,0:T(8,128)(2,1)S(1)} %get-tuple-element.152.refs_1_.refs_5_, bf16[384,128]{1,0:T(8,128)(2,1)S(1)} %get-tuple-element.112.refs_1_.refs_2_, ...), custom_call_target="tpu_custom_call" | custom-call | flops 1 | bytes 1 | tf_op jit(solution)/shard_map/pallas_call | solution.py:26
  204.1 7.0 %collective-permute-done.49.refs_2_ = bf16[64,1024]{1,0:T(8,128)(2,1)S(1)} collective-permute-done((bf16[64,1024]{1,0:T(8,128)(2,1)S(1)}, bf16[64,1024]{1,0:T(8,128)(2,1)S(1)}, u32[]{:S(2)}, u32[]{:S(2)}) %collective-permute-start.49) | collective-permute-done | bytes 131104 | tf_op jit(solution)/shard_map/ppermute | solution.py:96
  214.5 1.7 shard_map.309.refs_3_
  219.3 4.3 %collective-permute-done.54.refs_2_ = bf16[192,512]{1,0:T(8,128)(2,1)S(1)} collective-permute-done((bf16[192,512]{1,0:T(8,128)(2,1)S(1)}, bf16[192,512]{1,0:T(8,128)(2,1)S(1)}, u32[]{:S(2)}, u32[]{:S(2)}) %collective-permute-start.54) | collective-permute-done | bytes 196640 | tf_op jit(solution)/shard_map/ppermute | solution.py:96
  224.3 3.0 %collective-permute-start.58 = (bf16[64,384]{1,0:T(8,128)(2,1)S(1)}, bf16[64,384]{1,0:T(8,128)(2,1)S(1)}, u32[]{:S(2)}, u32[]{:S(2)}) collective-permute-start(bf16[64,384]{1,0:T(8,128)(2,1)S(1)} %get-tuple-element.230), channel_id=1, source_target_pairs={{0,12},{4,8},{8,4},{12,0},{1,13},{5,9},{9,5},{13,1},{2,14},{6,10},... | collective-permute-start | bytes 147464 | tf_op jit(solution)/shard_map/ppermute | solution.py:96
  227.3 2.3 collective-permute-start.57
  230.3 2.8 collective-permute-done.57.refs_3_
  238.4 1.7 shard_map.313
  244.7 4.8 %collective-permute-done.61.refs_2_ = bf16[192,512]{1,0:T(8,128)(2,1)S(1)} collective-permute-done((bf16[192,512]{1,0:T(8,128)(2,1)S(1)}, bf16[192,512]{1,0:T(8,128)(2,1)S(1)}, u32[]{:S(2)}, u32[]{:S(2)}) %collective-permute-start.61) | collective-permute-done | bytes 196640 | tf_op jit(solution)/shard_map/ppermute | solution.py:96
  250.2 1.4 collective-permute-done.62.refs_4_
  251.6 1.9 shard_map.318
  254.7 3.2 %collective-permute-start.69 = (bf16[64,640]{1,0:T(8,128)(2,1)S(1)}, bf16[64,640]{1,0:T(8,128)(2,1)S(1)}, u32[]{:S(2)}, u32[]{:S(2)}) collective-permute-start(bf16[64,640]{1,0:T(8,128)(2,1)S(1)} %get-tuple-element.226), channel_id=1, source_target_pairs={{0,12},{4,8},{8,4},{12,0},{1,13},{5,9},{9,5},{13,1},{2,14},{6,10},... | collective-permute-start | bytes 245768 | tf_op jit(solution)/shard_map/ppermute | solution.py:96
  260.8 2.4 collective-permute-start.66
  263.2 1.5 collective-permute-done.71
  264.7 1.6 collective-permute-start.65
  266.3 2.7 collective-permute-start.64
  272.6 4.6 %collective-permute-done.72.refs_2_ = f32[40,128]{1,0:T(8,128)S(1)} collective-permute-done((f32[40,128]{1,0:T(8,128)S(1)}, f32[40,128]{1,0:T(8,128)S(1)}, u32[]{:S(2)}, u32[]{:S(2)}) %collective-permute-start.72) | collective-permute-done | bytes 20512 | tf_op jit(solution)/shard_map/ppermute | solution.py:96
  (250 shorter events, 82.8 us)
Async XLA Ops:
  1.6 16.2 %collective-permute-start.5 = (bf16[64,1024]{1,0:T(8,128)(2,1)S(1)}, bf16[64,1024]{1,0:T(8,128)(2,1)S(1)}, u32[]{:S(2)}, u32[]{:S(2)}) collective-permute-start(bf16[64,1024]{1,0:T(8,128)(2,1)S(1)} %pad_maximum_fusion.2.refs_1_), channel_id=1, source_target_pairs={{0,12},{4,8},{8,4},{12,0},{1,13},{5,9},{9,5},{13,1},{2,14},{6,10},... | collective-permute-start | bytes 393224 | tf_op jit(solution)/shard_map/ppermute | solution.py:96
  6.7 11.1 %collective-permute-start.4 = (bf16[64,1024]{1,0:T(8,128)(2,1)S(1)}, bf16[64,1024]{1,0:T(8,128)(2,1)S(1)}, u32[]{:S(2)}, u32[]{:S(2)}) collective-permute-start(bf16[64,1024]{1,0:T(8,128)(2,1)S(1)} %pad_maximum_fusion.2.refs_1_), channel_id=1, source_target_pairs={{0,8},{4,12},{8,0},{12,4},{1,9},{5,13},{9,1},{13,5},{2,10},{6,14},... | collective-permute-start | bytes 393224 | tf_op jit(solution)/shard_map/ppermute | solution.py:96
  6.7 10.0 %collective-permute-start.3 = (bf16[64,1024]{1,0:T(8,128)(2,1)S(1)}, bf16[64,1024]{1,0:T(8,128)(2,1)S(1)}, u32[]{:S(2)}, u32[]{:S(2)}) collective-permute-start(bf16[64,1024]{1,0:T(8,128)(2,1)S(1)} %pad_maximum_fusion.2.refs_1_), channel_id=1, source_target_pairs={{0,4},{4,0},{8,12},{12,8},{1,5},{5,1},{9,13},{13,9},{2,6},{6,2},{1... | collective-permute-start | bytes 393224 | tf_op jit(solution)/shard_map/ppermute | solution.py:96
  10.5 12.5 %collective-permute-start.1 = (bf16[784,128]{1,0:T(8,128)(2,1)S(1)}, bf16[784,128]{1,0:T(8,128)(2,1)S(1)}, u32[]{:S(2)}, u32[]{:S(2)}) collective-permute-start(bf16[784,128]{1,0:T(8,128)(2,1)S(1)} %shard_map.279.refs_1_), channel_id=1, source_target_pairs={{0,2},{1,3},{2,0},{3,1},{4,6},{5,7},{6,4},{7,5},{8,10},{9,11},{10,... | collective-permute-start | bytes 602120 | tf_op jit(solution)/shard_map/ppermute | solution.py:96
  12.2 20.7 %collective-permute-start = (bf16[784,128]{1,0:T(8,128)(2,1)S(1)}, bf16[784,128]{1,0:T(8,128)(2,1)S(1)}, u32[]{:S(2)}, u32[]{:S(2)}) collective-permute-start(bf16[784,128]{1,0:T(8,128)(2,1)S(1)} %shard_map.279.refs_1_), channel_id=1, source_target_pairs={{0,1},{1,0},{2,3},{3,2},{4,5},{5,4},{6,7},{7,6},{8,9},{9,8},{10,11... | collective-permute-start | bytes 602120 | tf_op jit(solution)/shard_map/ppermute | solution.py:96
  18.4 7.0 %collective-permute-start.10 = (bf16[64,640]{1,0:T(8,128)(2,1)S(1)}, bf16[64,640]{1,0:T(8,128)(2,1)S(1)}, u32[]{:S(2)}, u32[]{:S(2)}) collective-permute-start(bf16[64,640]{1,0:T(8,128)(2,1)S(1)} %shard_map.282.refs_1_), channel_id=1, source_target_pairs={{0,12},{4,8},{8,4},{12,0},{1,13},{5,9},{9,5},{13,1},{2,14},{6,10},... | collective-permute-start | bytes 245768 | tf_op jit(solution)/shard_map/ppermute | solution.py:96
  21.1 7.2 %collective-permute-start.9 = (bf16[64,640]{1,0:T(8,128)(2,1)S(1)}, bf16[64,640]{1,0:T(8,128)(2,1)S(1)}, u32[]{:S(2)}, u32[]{:S(2)}) collective-permute-start(bf16[64,640]{1,0:T(8,128)(2,1)S(1)} %shard_map.282.refs_1_), channel_id=1, source_target_pairs={{0,8},{4,12},{8,0},{12,4},{1,9},{5,13},{9,1},{13,5},{2,10},{6,14},... | collective-permute-start | bytes 245768 | tf_op jit(solution)/shard_map/ppermute | solution.py:96
  21.2 7.1 %collective-permute-start.8 = (bf16[64,640]{1,0:T(8,128)(2,1)S(1)}, bf16[64,640]{1,0:T(8,128)(2,1)S(1)}, u32[]{:S(2)}, u32[]{:S(2)}) collective-permute-start(bf16[64,640]{1,0:T(8,128)(2,1)S(1)} %shard_map.282.refs_1_), channel_id=1, source_target_pairs={{0,4},{4,0},{8,12},{12,8},{1,5},{5,1},{9,13},{13,9},{2,6},{6,2},{1... | collective-permute-start | bytes 245768 | tf_op jit(solution)/shard_map/ppermute | solution.py:96
  23.0 14.2 %collective-permute-start.7 = (bf16[192,1024]{1,0:T(8,128)(2,1)S(1)}, bf16[192,1024]{1,0:T(8,128)(2,1)S(1)}, u32[]{:S(2)}, u32[]{:S(2)}) collective-permute-start(bf16[192,1024]{1,0:T(8,128)(2,1)S(1)} %constant_dynamic-update-slice_fusion.refs_2_), channel_id=1, source_target_pairs={{0,16},{16,0},{1,17},{17,1},{2,18},{18,2},{3,19},{19,3},{4,20},{20... | collective-permute-start | bytes 1179656 | tf_op jit(solution)/shard_map/ppermute | solution.py:96
  25.4 7.9 %collective-permute-start.2 = (bf16[784,128]{1,0:T(8,128)(2,1)S(1)}, bf16[784,128]{1,0:T(8,128)(2,1)S(1)}, u32[]{:S(2)}, u32[]{:S(2)}) collective-permute-start(bf16[784,128]{1,0:T(8,128)(2,1)S(1)} %collective-permute-done.1.refs_3_), channel_id=1, source_target_pairs={{0,1},{1,0},{2,3},{3,2},{4,5},{5,4},{6,7},{7,6},{8,9},{9,8},{10,11... | collective-permute-start | bytes 602120 | tf_op jit(solution)/shard_map/ppermute | solution.py:96
  28.4 7.4 %collective-permute-start.6 = (bf16[64,1024]{1,0:T(8,128)(2,1)S(1)}, bf16[64,1024]{1,0:T(8,128)(2,1)}, u32[]{:S(2)}, u32[]{:S(2)}) collective-permute-start(bf16[64,1024]{1,0:T(8,128)(2,1)S(1)} %pad_maximum_fusion.2.refs_1_), channel_id=1, source_target_pairs={{0,16},{16,0},{1,17},{17,1},{2,18},{18,2},{3,19},{19,3},{4,20},{20... | collective-permute-start | bytes 393224 | tf_op jit(solution)/shard_map/ppermute | solution.py:96
  30.5 14.3 %collective-permute-start.15 = (bf16[64,1408]{1,0:T(8,128)(2,1)S(1)}, bf16[64,1408]{1,0:T(8,128)(2,1)S(1)}, u32[]{:S(2)}, u32[]{:S(2)}) collective-permute-start(bf16[64,1408]{1,0:T(8,128)(2,1)S(1)} %shard_map.284.refs_1_), channel_id=1, source_target_pairs={{0,12},{4,8},{8,4},{12,0},{1,13},{5,9},{9,5},{13,1},{2,14},{6,10},... | collective-permute-start | bytes 540680 | tf_op jit(solution)/shard_map/ppermute | solution.py:96
  33.0 15.8 %collective-permute-start.14 = (bf16[64,1408]{1,0:T(8,128)(2,1)S(1)}, bf16[64,1408]{1,0:T(8,128)(2,1)S(1)}, u32[]{:S(2)}, u32[]{:S(2)}) collective-permute-start(bf16[64,1408]{1,0:T(8,128)(2,1)S(1)} %shard_map.284.refs_1_), channel_id=1, source_target_pairs={{0,8},{4,12},{8,0},{12,4},{1,9},{5,13},{9,1},{13,5},{2,10},{6,14},... | collective-permute-start | bytes 540680 | tf_op jit(solution)/shard_map/ppermute | solution.py:96
  33.3 15.5 %collective-permute-start.13 = (bf16[64,1408]{1,0:T(8,128)(2,1)S(1)}, bf16[64,1408]{1,0:T(8,128)(2,1)S(1)}, u32[]{:S(2)}, u32[]{:S(2)}) collective-permute-start(bf16[64,1408]{1,0:T(8,128)(2,1)S(1)} %shard_map.284.refs_1_), channel_id=1, source_target_pairs={{0,4},{4,0},{8,12},{12,8},{1,5},{5,1},{9,13},{13,9},{2,6},{6,2},{1... | collective-permute-start | bytes 540680 | tf_op jit(solution)/shard_map/ppermute | solution.py:96
  35.8 14.0 %collective-permute-start.16 = (bf16[256,640]{1,0:T(8,128)(2,1)S(1)}, bf16[256,640]{1,0:T(8,128)(2,1)S(1)}, u32[]{:S(2)}, u32[]{:S(2)}) collective-permute-start(bf16[256,640]{1,0:T(8,128)(2,1)S(1)} %pad_maximum_fusion.1.refs_4_.refs_2_), channel_id=1, source_target_pairs={{0,16},{16,0},{1,17},{17,1},{2,18},{18,2},{3,19},{19,3},{4,20},{20... | collective-permute-start | bytes 983048 | tf_op jit(solution)/shard_map/ppermute | solution.py:96
  44.8 4.8 %collective-permute-start.11 = (bf16[192,512]{1,0:T(8,128)(2,1)S(1)}, bf16[192,512]{1,0:T(8,128)(2,1)S(1)}, u32[]{:S(2)}, u32[]{:S(2)}) collective-permute-start(bf16[192,512]{1,0:T(8,128)(2,1)S(1)} %get-tuple-element.108), channel_id=1, source_target_pairs={{0,1},{1,0},{2,3},{3,2},{4,5},{5,4},{6,7},{7,6},{8,9},{9,8},{10,11... | collective-permute-start | bytes 589832 | tf_op jit(solution)/shard_map/ppermute | solution.py:96
  48.8 16.9 %collective-permute-start.21 = (bf16[256,1408]{1,0:T(8,128)(2,1)S(1)}, bf16[256,1408]{1,0:T(8,128)(2,1)S(1)}, u32[]{:S(2)}, u32[]{:S(2)}) collective-permute-start(bf16[256,1408]{1,0:T(8,128)(2,1)S(1)} %pad_maximum_fusion.refs_3_), channel_id=1, source_target_pairs={{0,16},{16,0},{1,17},{17,1},{2,18},{18,2},{3,19},{19,3},{4,20},{20... | collective-permute-start | bytes 2162696 | tf_op jit(solution)/shard_map/ppermute | solution.py:96
  49.7 5.7 %collective-permute-start.12 = (bf16[192,512]{1,0:T(8,128)(2,1)S(1)}, bf16[192,512]{1,0:T(8,128)(2,1)S(1)}, u32[]{:S(2)}, u32[]{:S(2)}) collective-permute-start(bf16[192,512]{1,0:T(8,128)(2,1)S(1)} %add_convert_fusion.9.refs_1_), channel_id=1, source_target_pairs={{0,2},{1,3},{2,0},{3,1},{4,6},{5,7},{6,4},{7,5},{8,10},{9,11},{10,... | collective-permute-start | bytes 589832 | tf_op jit(solution)/shard_map/ppermute | solution.py:96
  58.8 10.7 %collective-permute-start.20 = (bf16[384,256]{1,0:T(8,128)(2,1)S(1)}, bf16[384,256]{1,0:T(8,128)(2,1)S(1)}, u32[]{:S(2)}, u32[]{:S(2)}) collective-permute-start(bf16[384,256]{1,0:T(8,128)(2,1)S(1)} %get-tuple-element.111.refs_2_.refs_9_), channel_id=1, source_target_pairs={{0,12},{4,8},{8,4},{12,0},{1,13},{5,9},{9,5},{13,1},{2,14},{6,10},... | collective-permute-start | bytes 589832 | tf_op jit(solution)/shard_map/ppermute | solution.py:96
  60.3 17.0 %collective-permute-start.19 = (bf16[384,256]{1,0:T(8,128)(2,1)S(1)}, bf16[384,256]{1,0:T(8,128)(2,1)S(1)}, u32[]{:S(2)}, u32[]{:S(2)}) collective-permute-start(bf16[384,256]{1,0:T(8,128)(2,1)S(1)} %get-tuple-element.111.refs_2_.refs_9_), channel_id=1, source_target_pairs={{0,8},{4,12},{8,0},{12,4},{1,9},{5,13},{9,1},{13,5},{2,10},{6,14},... | collective-permute-start | bytes 589832 | tf_op jit(solution)/shard_map/ppermute | solution.py:96
  60.3 17.0 %collective-permute-start.18 = (bf16[384,256]{1,0:T(8,128)(2,1)S(1)}, bf16[384,256]{1,0:T(8,128)(2,1)S(1)}, u32[]{:S(2)}, u32[]{:S(2)}) collective-permute-start(bf16[384,256]{1,0:T(8,128)(2,1)S(1)} %get-tuple-element.111.refs_2_.refs_9_), channel_id=1, source_target_pairs={{0,4},{4,0},{8,12},{12,8},{1,5},{5,1},{9,13},{13,9},{2,6},{6,2},{1... | collective-permute-start | bytes 589832 | tf_op jit(solution)/shard_map/ppermute | solution.py:96
  81.9 1.5 collective-permute-start.22
  83.4 7.0 %collective-permute-start.23 = (bf16[192,512]{1,0:T(8,128)(2,1)S(1)}, bf16[192,512]{1,0:T(8,128)(2,1)S(1)}, u32[]{:S(2)}, u32[]{:S(2)}) collective-permute-start(bf16[192,512]{1,0:T(8,128)(2,1)S(1)} %add_convert_fusion.8), channel_id=1, source_target_pairs={{0,2},{1,3},{2,0},{3,1},{4,6},{5,7},{6,4},{7,5},{8,10},{9,11},{10,... | collective-permute-start | bytes 589832 | tf_op jit(solution)/shard_map/ppermute | solution.py:96
  93.4 2.7 collective-permute-start.25
  94.8 5.5 %collective-permute-start.26 = (bf16[16,128]{1,0:T(8,128)(2,1)S(1)}, bf16[16,128]{1,0:T(8,128)(2,1)S(1)}, u32[]{:S(2)}, u32[]{:S(2)}) collective-permute-start(bf16[16,128]{1,0:T(8,128)(2,1)S(1)} %get-tuple-element.119), channel_id=1, source_target_pairs={{4,0},{8,4},{12,8},{5,1},{9,5},{13,9},{6,2},{10,6},{14,10},{7,3},{... | collective-permute-start | bytes 12296 | tf_op jit(solution)/shard_map/ppermute | solution.py:682
  101.6 3.7 %collective-permute-start.27 = (f32[8,128]{1,0:T(8,128)S(1)}, f32[8,128]{1,0:T(8,128)S(1)}, u32[]{:S(2)}, u32[]{:S(2)}) collective-permute-start(f32[8,128]{1,0:T(8,128)S(1)} %get-tuple-element.121), channel_id=1, source_target_pairs={{0,16},{16,0},{1,17},{17,1},{2,18},{18,2},{3,19},{19,3},{4,20},{20... | collective-permute-start | bytes 12296 | tf_op jit(solution)/shard_map/ppermute | solution.py:96
  105.2 3.7 %collective-permute-start.28 = (f32[8,128]{1,0:T(8,128)S(1)}, f32[8,128]{1,0:T(8,128)S(1)}, u32[]{:S(2)}, u32[]{:S(2)}) collective-permute-start(f32[8,128]{1,0:T(8,128)S(1)} %maximum_maximum_fusion), channel_id=1, source_target_pairs={{0,4},{4,0},{8,12},{12,8},{1,5},{5,1},{9,13},{13,9},{2,6},{6,2},{1... | collective-permute-start | bytes 12296 | tf_op jit(solution)/shard_map/ppermute | solution.py:96
  108.9 5.0 %collective-permute-start.29 = (f32[8,128]{1,0:T(8,128)S(1)}, f32[8,128]{1,0:T(8,128)S(1)}, u32[]{:S(2)}, u32[]{:S(2)}) collective-permute-start(f32[8,128]{1,0:T(8,128)S(1)} %maximum_maximum_fusion.1), channel_id=1, source_target_pairs={{0,8},{4,12},{8,0},{12,4},{1,9},{5,13},{9,1},{13,5},{2,10},{6,14},... | collective-permute-start | bytes 12296 | tf_op jit(solution)/shard_map/ppermute | solution.py:96
  116.4 7.0 %collective-permute-start.31 = (bf16[192,512]{1,0:T(8,128)(2,1)S(1)}, bf16[192,512]{1,0:T(8,128)(2,1)S(1)}, u32[]{:S(2)}, u32[]{:S(2)}) collective-permute-start(bf16[192,512]{1,0:T(8,128)(2,1)S(1)} %add_convert_fusion.6), channel_id=1, source_target_pairs={{0,2},{1,3},{2,0},{3,1},{4,6},{5,7},{6,4},{7,5},{8,10},{9,11},{10,... | collective-permute-start | bytes 589832 | tf_op jit(solution)/shard_map/ppermute | solution.py:96
  126.5 1.5 collective-permute-start.33
  128.1 7.0 %collective-permute-start.34 = (bf16[192,512]{1,0:T(8,128)(2,1)S(1)}, bf16[192,512]{1,0:T(8,128)(2,1)S(1)}, u32[]{:S(2)}, u32[]{:S(2)}) collective-permute-start(bf16[192,512]{1,0:T(8,128)(2,1)S(1)} %add_convert_fusion.4), channel_id=1, source_target_pairs={{0,2},{1,3},{2,0},{3,1},{4,6},{5,7},{6,4},{7,5},{8,10},{9,11},{10,... | collective-permute-start | bytes 589832 | tf_op jit(solution)/shard_map/ppermute | solution.py:96
  135.2 1.5 collective-permute-start.35
  140.5 7.0 %collective-permute-start.37 = (bf16[192,512]{1,0:T(8,128)(2,1)S(1)}, bf16[192,512]{1,0:T(8,128)(2,1)S(1)}, u32[]{:S(2)}, u32[]{:S(2)}) collective-permute-start(bf16[192,512]{1,0:T(8,128)(2,1)S(1)} %add_convert_fusion.2.refs_1_), channel_id=1, source_target_pairs={{0,2},{1,3},{2,0},{3,1},{4,6},{5,7},{6,4},{7,5},{8,10},{9,11},{10,... | collective-permute-start | bytes 589832 | tf_op jit(solution)/shard_map/ppermute | solution.py:96
  150.9 3.7 %collective-permute-start.39 = (f32[8,128]{1,0:T(8,128)S(1)}, f32[8,128]{1,0:T(8,128)S(1)}, u32[]{:S(2)}, u32[]{:S(2)}) collective-permute-start(f32[8,128]{1,0:T(8,128)S(1)} %slice.148), channel_id=1, source_target_pairs={{0,16},{16,0},{1,17},{17,1},{2,18},{18,2},{3,19},{19,3},{4,20},{20... | collective-permute-start | bytes 12296 | tf_op jit(solution)/shard_map/ppermute | solution.py:96
  151.9 13.8 %collective-permute-start.42 = (bf16[256,1024]{1,0:T(8,128)(2,1)S(1)}, bf16[256,1024]{1,0:T(8,128)(2,1)S(1)}, u32[]{:S(2)}, u32[]{:S(2)}) collective-permute-start(bf16[256,1024]{1,0:T(8,128)(2,1)S(1)} %get-tuple-element.213), channel_id=1, source_target_pairs={{0,16},{16,0},{1,17},{17,1},{2,18},{18,2},{3,19},{19,3},{4,20},{20... | collective-permute-start | bytes 1572872 | tf_op jit(solution)/shard_map/ppermute | solution.py:96
  154.6 4.0 %collective-permute-start.40 = (f32[72,128]{1,0:T(8,128)S(1)}, f32[72,128]{1,0:T(8,128)S(1)}, u32[]{:S(2)}, u32[]{:S(2)}) collective-permute-start(f32[72,128]{1,0:T(8,128)S(1)} %pad_maximum_fusion.3), channel_id=1, source_target_pairs={{0,4},{4,0},{8,12},{12,8},{1,5},{5,1},{9,13},{13,9},{2,6},{6,2},{1... | collective-permute-start | bytes 110600 | tf_op jit(solution)/shard_map/ppermute | solution.py:96
  158.6 7.0 %collective-permute-start.41 = (f32[72,128]{1,0:T(8,128)S(1)}, f32[72,128]{1,0:T(8,128)S(1)}, u32[]{:S(2)}, u32[]{:S(2)}) collective-permute-start(f32[72,128]{1,0:T(8,128)S(1)} %pad_maximum_fusion.4.refs_3_), channel_id=1, source_target_pairs={{0,12},{4,8},{8,4},{12,0},{1,13},{5,9},{9,5},{13,1},{2,14},{6,10},... | collective-permute-start | bytes 110600 | tf_op jit(solution)/shard_map/ppermute | solution.py:96
  167.1 2.1 collective-permute-start.43
  169.3 7.4 %collective-permute-start.44 = (bf16[192,512]{1,0:T(8,128)(2,1)S(1)}, bf16[192,512]{1,0:T(8,128)(2,1)S(1)}, u32[]{:S(2)}, u32[]{:S(2)}) collective-permute-start(bf16[192,512]{1,0:T(8,128)(2,1)S(1)} %add_convert_fusion.1.refs_3_.refs_1_), channel_id=1, source_target_pairs={{0,2},{1,3},{2,0},{3,1},{4,6},{5,7},{6,4},{7,5},{8,10},{9,11},{10,... | collective-permute-start | bytes 589832 | tf_op jit(solution)/shard_map/ppermute | solution.py:96
  170.6 26.3 %collective-permute-start.51 = (bf16[64,1024]{1,0:T(8,128)(2,1)S(1)}, bf16[64,1024]{1,0:T(8,128)(2,1)S(1)}, u32[]{:S(2)}, u32[]{:S(2)}) collective-permute-start(bf16[64,1024]{1,0:T(8,128)(2,1)S(1)} %get-tuple-element.220), channel_id=1, source_target_pairs={{0,12},{4,8},{8,4},{12,0},{1,13},{5,9},{9,5},{13,1},{2,14},{6,10},... | collective-permute-start | bytes 393224 | tf_op jit(solution)/shard_map/ppermute | solution.py:96
  173.0 25.3 %collective-permute-start.50 = (bf16[64,1024]{1,0:T(8,128)(2,1)S(1)}, bf16[64,1024]{1,0:T(8,128)(2,1)S(1)}, u32[]{:S(2)}, u32[]{:S(2)}) collective-permute-start(bf16[64,1024]{1,0:T(8,128)(2,1)S(1)} %get-tuple-element.221), channel_id=1, source_target_pairs={{0,8},{4,12},{8,0},{12,4},{1,9},{5,13},{9,1},{13,5},{2,10},{6,14},... | collective-permute-start | bytes 393224 | tf_op jit(solution)/shard_map/ppermute | solution.py:96
  177.4 35.1 %collective-permute-start.52 = (bf16[256,384]{1,0:T(8,128)(2,1)S(1)}, bf16[256,384]{1,0:T(8,128)(2,1)S(1)}, u32[]{:S(2)}, u32[]{:S(2)}) collective-permute-start(bf16[256,384]{1,0:T(8,128)(2,1)S(1)} %get-tuple-element.225), channel_id=1, source_target_pairs={{0,16},{16,0},{1,17},{17,1},{2,18},{18,2},{3,19},{19,3},{4,20},{20... | collective-permute-start | bytes 589832 | tf_op jit(solution)/shard_map/ppermute | solution.py:96
  193.8 18.6 %collective-permute-start.46 = (bf16[384,256]{1,0:T(8,128)(2,1)S(1)}, bf16[384,256]{1,0:T(8,128)(2,1)S(1)}, u32[]{:S(2)}, u32[]{:S(2)}) collective-permute-start(bf16[384,256]{1,0:T(8,128)(2,1)S(1)} %get-tuple-element.155), channel_id=1, source_target_pairs={{0,4},{4,0},{8,12},{12,8},{1,5},{5,1},{9,13},{13,9},{2,6},{6,2},{1... | collective-permute-start | bytes 589832 | tf_op jit(solution)/shard_map/ppermute | solution.py:96
  195.4 17.1 %collective-permute-start.47 = (bf16[384,256]{1,0:T(8,128)(2,1)S(1)}, bf16[384,256]{1,0:T(8,128)(2,1)S(1)}, u32[]{:S(2)}, u32[]{:S(2)}) collective-permute-start(bf16[384,256]{1,0:T(8,128)(2,1)S(1)} %get-tuple-element.156), channel_id=1, source_target_pairs={{0,8},{4,12},{8,0},{12,4},{1,9},{5,13},{9,1},{13,5},{2,10},{6,14},... | collective-permute-start | bytes 589832 | tf_op jit(solution)/shard_map/ppermute | solution.py:96
  196.9 15.6 %collective-permute-start.48 = (bf16[384,256]{1,0:T(8,128)(2,1)S(1)}, bf16[384,256]{1,0:T(8,128)(2,1)S(1)}, u32[]{:S(2)}, u32[]{:S(2)}) collective-permute-start(bf16[384,256]{1,0:T(8,128)(2,1)S(1)} %get-tuple-element.157), channel_id=1, source_target_pairs={{0,12},{4,8},{8,4},{12,0},{1,13},{5,9},{9,5},{13,1},{2,14},{6,10},... | collective-permute-start | bytes 589832 | tf_op jit(solution)/shard_map/ppermute | solution.py:96
  198.3 12.9 %collective-permute-start.49 = (bf16[64,1024]{1,0:T(8,128)(2,1)S(1)}, bf16[64,1024]{1,0:T(8,128)(2,1)S(1)}, u32[]{:S(2)}, u32[]{:S(2)}) collective-permute-start(bf16[64,1024]{1,0:T(8,128)(2,1)S(1)} %get-tuple-element.222), channel_id=1, source_target_pairs={{0,4},{4,0},{8,12},{12,8},{1,5},{5,1},{9,13},{13,9},{2,6},{6,2},{1... | collective-permute-start | bytes 393224 | tf_op jit(solution)/shard_map/ppermute | solution.py:96
  214.4 1.8 collective-permute-start.53
  216.2 7.4 %collective-permute-start.54 = (bf16[192,512]{1,0:T(8,128)(2,1)S(1)}, bf16[192,512]{1,0:T(8,128)(2,1)S(1)}, u32[]{:S(2)}, u32[]{:S(2)}) collective-permute-start(bf16[192,512]{1,0:T(8,128)(2,1)S(1)} %add_convert_fusion.refs_3_.refs_1_.refs_5_), channel_id=1, source_target_pairs={{0,2},{1,3},{2,0},{3,1},{4,6},{5,7},{6,4},{7,5},{8,10},{9,11},{10,... | collective-permute-start | bytes 589832 | tf_op jit(solution)/shard_map/ppermute | solution.py:96
  217.6 24.0 %collective-permute-start.60 = (bf16[256,640]{1,0:T(8,128)(2,1)}, bf16[256,640]{1,0:T(8,128)(2,1)S(1)}, u32[]{:S(2)}, u32[]{:S(2)}) collective-permute-start(bf16[256,640]{1,0:T(8,128)(2,1)} %get-tuple-element.215), channel_id=1, source_target_pairs={{0,16},{16,0},{1,17},{17,1},{2,18},{18,2},{3,19},{19,3},{4,20},{20... | collective-permute-start | bytes 983048 | tf_op jit(solution)/shard_map/ppermute | solution.py:96
  224.2 11.9 %collective-permute-start.55 = (bf16[192,512]{1,0:T(8,128)(2,1)S(1)}, bf16[192,512]{1,0:T(8,128)(2,1)S(1)}, u32[]{:S(2)}, u32[]{:S(2)}) collective-permute-start(bf16[192,512]{1,0:T(8,128)(2,1)S(1)} %shard_map.311.refs_3_), channel_id=1, source_target_pairs={{0,1},{1,0},{2,3},{3,2},{4,5},{5,4},{6,7},{7,6},{8,9},{9,8},{10,11... | collective-permute-start | bytes 589832 | tf_op jit(solution)/shard_map/ppermute | solution.py:96
  224.3 6.0 %collective-permute-start.58 = (bf16[64,384]{1,0:T(8,128)(2,1)S(1)}, bf16[64,384]{1,0:T(8,128)(2,1)S(1)}, u32[]{:S(2)}, u32[]{:S(2)}) collective-permute-start(bf16[64,384]{1,0:T(8,128)(2,1)S(1)} %get-tuple-element.230), channel_id=1, source_target_pairs={{0,12},{4,8},{8,4},{12,0},{1,13},{5,9},{9,5},{13,1},{2,14},{6,10},... | collective-permute-start | bytes 147464 | tf_op jit(solution)/shard_map/ppermute | solution.py:96
  227.3 5.8 %collective-permute-start.57 = (bf16[64,384]{1,0:T(8,128)(2,1)S(1)}, bf16[64,384]{1,0:T(8,128)(2,1)S(1)}, u32[]{:S(2)}, u32[]{:S(2)}) collective-permute-start(bf16[64,384]{1,0:T(8,128)(2,1)S(1)} %get-tuple-element.231), channel_id=1, source_target_pairs={{0,8},{4,12},{8,0},{12,4},{1,9},{5,13},{9,1},{13,5},{2,10},{6,14},... | collective-permute-start | bytes 147464 | tf_op jit(solution)/shard_map/ppermute | solution.py:96
  229.6 4.4 %collective-permute-start.56 = (bf16[64,384]{1,0:T(8,128)(2,1)S(1)}, bf16[64,384]{1,0:T(8,128)(2,1)S(1)}, u32[]{:S(2)}, u32[]{:S(2)}) collective-permute-start(bf16[64,384]{1,0:T(8,128)(2,1)S(1)} %get-tuple-element.232), channel_id=1, source_target_pairs={{0,4},{4,0},{8,12},{12,8},{1,5},{5,1},{9,13},{13,9},{2,6},{6,2},{1... | collective-permute-start | bytes 147464 | tf_op jit(solution)/shard_map/ppermute | solution.py:96
  242.2 7.3 %collective-permute-start.61 = (bf16[192,512]{1,0:T(8,128)(2,1)S(1)}, bf16[192,512]{1,0:T(8,128)(2,1)S(1)}, u32[]{:S(2)}, u32[]{:S(2)}) collective-permute-start(bf16[192,512]{1,0:T(8,128)(2,1)S(1)} %shard_map.315.refs_3_.refs_1_), channel_id=1, source_target_pairs={{0,2},{1,3},{2,0},{3,1},{4,6},{5,7},{6,4},{7,5},{8,10},{9,11},{10,... | collective-permute-start | bytes 589832 | tf_op jit(solution)/shard_map/ppermute | solution.py:96
  242.8 16.3 %collective-permute-start.63 = (bf16[256,1024]{1,0:T(8,128)(2,1)S(1)}, bf16[256,1024]{1,0:T(8,128)(2,1)S(1)}, u32[]{:S(2)}, u32[]{:S(2)}) collective-permute-start(bf16[256,1024]{1,0:T(8,128)(2,1)S(1)} %get-tuple-element.210), channel_id=1, source_target_pairs={{0,16},{16,0},{1,17},{17,1},{2,18},{18,2},{3,19},{19,3},{4,20},{20... | collective-permute-start | bytes 1572872 | tf_op jit(solution)/shard_map/ppermute | solution.py:96
  253.5 6.3 %collective-permute-start.70 = (f32[40,128]{1,0:T(8,128)S(1)}, f32[40,128]{1,0:T(8,128)S(1)}, u32[]{:S(2)}, u32[]{:S(2)}) collective-permute-start(f32[40,128]{1,0:T(8,128)S(1)} %get-tuple-element.182.refs_3_), channel_id=1, source_target_pairs={{0,16},{16,0},{1,17},{17,1},{2,18},{18,2},{3,19},{19,3},{4,20},{20... | collective-permute-start | bytes 61448 | tf_op jit(solution)/shard_map/ppermute | solution.py:96
  254.7 11.6 %collective-permute-start.69 = (bf16[64,640]{1,0:T(8,128)(2,1)S(1)}, bf16[64,640]{1,0:T(8,128)(2,1)S(1)}, u32[]{:S(2)}, u32[]{:S(2)}) collective-permute-start(bf16[64,640]{1,0:T(8,128)(2,1)S(1)} %get-tuple-element.226), channel_id=1, source_target_pairs={{0,12},{4,8},{8,4},{12,0},{1,13},{5,9},{9,5},{13,1},{2,14},{6,10},... | collective-permute-start | bytes 245768 | tf_op jit(solution)/shard_map/ppermute | solution.py:96
  257.9 12.2 %collective-permute-start.68 = (bf16[64,640]{1,0:T(8,128)(2,1)S(1)}, bf16[64,640]{1,0:T(8,128)(2,1)S(1)}, u32[]{:S(2)}, u32[]{:S(2)}) collective-permute-start(bf16[64,640]{1,0:T(8,128)(2,1)S(1)} %get-tuple-element.227), channel_id=1, source_target_pairs={{0,8},{4,12},{8,0},{12,4},{1,9},{5,13},{9,1},{13,5},{2,10},{6,14},... | collective-permute-start | bytes 245768 | tf_op jit(solution)/shard_map/ppermute | solution.py:96
  257.9 13.5 %collective-permute-start.67 = (bf16[64,640]{1,0:T(8,128)(2,1)S(1)}, bf16[64,640]{1,0:T(8,128)(2,1)S(1)}, u32[]{:S(2)}, u32[]{:S(2)}) collective-permute-start(bf16[64,640]{1,0:T(8,128)(2,1)S(1)} %get-tuple-element.228), channel_id=1, source_target_pairs={{0,4},{4,0},{8,12},{12,8},{1,5},{5,1},{9,13},{13,9},{2,6},{6,2},{1... | collective-permute-start | bytes 245768 | tf_op jit(solution)/shard_map/ppermute | solution.py:96
  259.8 4.9 %collective-permute-start.71 = (f32[40,128]{1,0:T(8,128)S(1)}, f32[40,128]{1,0:T(8,128)S(1)}, u32[]{:S(2)}, u32[]{:S(2)}) collective-permute-start(f32[40,128]{1,0:T(8,128)S(1)} %add.125), channel_id=1, source_target_pairs={{0,4},{4,0},{8,12},{12,8},{1,5},{5,1},{9,13},{13,9},{2,6},{6,2},{1... | collective-permute-start | bytes 61448 | tf_op jit(solution)/shard_map/ppermute | solution.py:96
  260.8 17.7 %collective-permute-start.66 = (bf16[64,1024]{1,0:T(8,128)(2,1)S(1)}, bf16[64,1024]{1,0:T(8,128)(2,1)S(1)}, u32[]{:S(2)}, u32[]{:S(2)}) collective-permute-start(bf16[64,1024]{1,0:T(8,128)(2,1)S(1)} %get-tuple-element.216), channel_id=1, source_target_pairs={{0,12},{4,8},{8,4},{12,0},{1,13},{5,9},{9,5},{13,1},{2,14},{6,10},... | collective-permute-start | bytes 393224 | tf_op jit(solution)/shard_map/ppermute | solution.py:96
  264.7 13.8 %collective-permute-start.65 = (bf16[64,1024]{1,0:T(8,128)(2,1)S(1)}, bf16[64,1024]{1,0:T(8,128)(2,1)S(1)}, u32[]{:S(2)}, u32[]{:S(2)}) collective-permute-start(bf16[64,1024]{1,0:T(8,128)(2,1)S(1)} %get-tuple-element.217), channel_id=1, source_target_pairs={{0,8},{4,12},{8,0},{12,4},{1,9},{5,13},{9,1},{13,5},{2,10},{6,14},... | collective-permute-start | bytes 393224 | tf_op jit(solution)/shard_map/ppermute | solution.py:96
  266.3 12.2 %collective-permute-start.64 = (bf16[64,1024]{1,0:T(8,128)(2,1)S(1)}, bf16[64,1024]{1,0:T(8,128)(2,1)S(1)}, u32[]{:S(2)}, u32[]{:S(2)}) collective-permute-start(bf16[64,1024]{1,0:T(8,128)(2,1)S(1)} %get-tuple-element.218), channel_id=1, source_target_pairs={{0,4},{4,0},{8,12},{12,8},{1,5},{5,1},{9,13},{13,9},{2,6},{6,2},{1... | collective-permute-start | bytes 393224 | tf_op jit(solution)/shard_map/ppermute | solution.py:96
  270.2 7.1 %collective-permute-start.72 = (f32[40,128]{1,0:T(8,128)S(1)}, f32[40,128]{1,0:T(8,128)S(1)}, u32[]{:S(2)}, u32[]{:S(2)}) collective-permute-start(f32[40,128]{1,0:T(8,128)S(1)} %add.126.refs_1_), channel_id=1, source_target_pairs={{0,8},{4,12},{8,0},{12,4},{1,9},{5,13},{9,1},{13,5},{2,10},{6,14},... | collective-permute-start | bytes 61448 | tf_op jit(solution)/shard_map/ppermute | solution.py:96
  (40 other events, 235.0 us)
